TPU v7x, 32 devices: a whole 2x2x4 slice. The times are simulated.
32 devices in a mesh: dp: 16 (over z, y, core), replica: 2 (over x).
Axes of the slice: x: 2, y: 2, z: 4, core: 2. Of those that a mesh axis runs over, the one named last changes fastest.
Arguments:
- img_emb: bfloat16 [2, 2048, 768], P('replica', 'dp')
- txt_base: bfloat16 [2, 2048, 768], P('replica', 'dp')
- txt_feat: bfloat16 [2, 2048, 640], P('replica', 'dp'), may hold values from -6 to 6
- head: float32 [640, 768], P('dp'), may hold values from -0.25 to 0.25
- momentum: float32 [640, 768], P('dp'), may hold values from -3 to 3
- positive_image: int32 [2, 2048], P('replica', 'dp'), may hold values from 0 to 2047, each once within a row
Outputs:
- new_head: float32 [640, 768], P('dp')
- new_momentum: float32 [640, 768], P('dp')
Inputs may be any that keep to these rules, and one draw needn't show every extreme that they name: `positive_image`: in each replica the 2048 texts name 2048 different images.
All inputs are finite; a program needn't handle non-finite values.
Results may differ from a plain program's by a relative error of at most 0.005.
Values may be sent and summed in bfloat16 or wider, within the bound.
No kernel may reach another device: no remote copies, remote signals or barrier semaphores. Data moves between devices by JAX's collectives and lax.ppermute only.
A program may use at most 64 MiB of HBM per device.

v0:
```python
import jax
import jax.numpy as jnp
from jax import lax
from jax.sharding import PartitionSpec as P

logit_scale = 10.0
logit_bias = -3.0
norm_epsilon = 1e-06
momentum_decay = 0.9
blend_weight = 0.7
outer_rate = 0.7


def per_device(img_emb, txt_base, txt_feat, head, momentum, positive_image):
    features = txt_feat[0]
    labels = positive_image[0]
    image_wide = img_emb[0].astype(jnp.float32)
    image_unit = (
        image_wide
        * lax.rsqrt(jnp.sum(image_wide * image_wide, axis=1, keepdims=True) + norm_epsilon)
    ).astype(jnp.bfloat16)
    head_low = head.astype(jnp.bfloat16)
    columns = features
    projected = jnp.dot(
        columns,
        lax.all_gather(head_low, "dp", axis=0, tiled=True),
        preferred_element_type=jnp.float32,
    )
    text_emb = txt_base[0].astype(jnp.float32) + projected
    inv_norm = lax.rsqrt(jnp.sum(text_emb * text_emb, axis=1, keepdims=True) + norm_epsilon)
    text_exact = text_emb * inv_norm
    text_unit = text_exact.astype(jnp.bfloat16)
    piece = lax.all_gather(image_unit, "dp", axis=0, tiled=True)
    logits = (
        logit_scale
        * lax.dot_general(
            text_unit, piece, (((1,), (1,)), ((), ())), preferred_element_type=jnp.float32
        )
        + logit_bias
    )
    columns = lax.iota(jnp.int32, piece.shape[0])
    matches = (labels[:, None] == columns[None, :]).astype(jnp.float32)
    weights = (jax.nn.sigmoid(logits) - matches).astype(jnp.bfloat16)
    unit_grad = logit_scale * jnp.dot(weights, piece, preferred_element_type=jnp.float32)
    along = jnp.sum(text_exact * unit_grad, axis=1, keepdims=True)
    text_grad = ((unit_grad - text_exact * along) * inv_norm).astype(jnp.bfloat16)
    share_rows = head.shape[0]
    local_term = lax.dot_general(
        features, text_grad, (((0,), (0,)), ((), ())), preferred_element_type=jnp.float32
    )
    summed = lax.psum(local_term, ("dp", "replica"))
    share = lax.dynamic_slice_in_dim(summed, lax.axis_index("dp") * share_rows, share_rows, 0)
    head_grad = share / lax.axis_size("replica")
    new_momentum = momentum_decay * momentum + (1.0 - momentum_decay) * head_grad
    new_head = head - outer_rate * ((1.0 - blend_weight) * head_grad + blend_weight * new_momentum)
    return (new_head, new_momentum)


def solution(mesh):
    placed = (
        P("replica", "dp", None),
        P("replica", "dp", None),
        P("replica", "dp", None),
        P("dp", None),
        P("dp", None),
        P("replica", "dp"),
    )
    return jax.shard_map(
        per_device,
        mesh=mesh,
        in_specs=placed,
        out_specs=(P("dp", None), P("dp", None)),
        check_vma=False,
    )
```

profile of v0, /device:TPU:0, one launch (start us, length us, event | category | flops | bytes accessed | tf_op | source)
XLA Modules:
  0.0 208.0 jit_solution(1546080865747815465)
XLA Ops:
  7.2 0.0 copy-start
  7.2 0.0 copy-start.3
  7.2 0.0 all-gather.2.cloned.1.call-start
  7.2 1.1 fusion.11
  8.3 1.7 fusion.12
  10.1 0.0 all-gather.2.cloned.1.call-update
  10.1 0.0 all-reduce.2.cloned.1.call-start
  10.1 0.9 convert_element_type.32
  11.0 27.3 %all_gather.6 = bf16[640,768]{1,0:T(8,128)(2,1)S(1)} all-gather(bf16[40,768]{1,0:T(8,128)(2,1)S(1)} %convert_element_type.32), channel_id=1, replica_groups=mesh['dp'=16,'replica'=2] {'dp'}, dimensions={0}, use_global_device_ids=true | all-gather | bytes 1044480 | tf_op jit(solution)/shard_map/all_gather | solution.py:26
  38.4 0.0 copy-done
  38.4 1.4 multiply_reduce_fusion.1
  39.7 21.0 %all-gather.2.cloned.1.call-done = bf16[2048,768]{1,0:T(8,128)(2,1)} async-done(((bf16[128,768]{1,0:T(8,128)(2,1)}), bf16[2048,768]{1,0:T(8,128)(2,1)}) %all-gather.2.cloned.1.call-update) | async-done | bytes 3145744 | tf_op jit(solution)/shard_map/all_gather | solution.py:33
  60.7 0.0 copy-done.3
  60.8 4.6 %multiply_reduce_fusion = (f32[128]{0:T(128)S(1)}, f32[128,768]{1,0:T(8,128)S(1)}) fusion(f32[128,768]{1,0:T(8,128)S(1)} %get-tuple-element.7, f32[128]{0:T(128)S(1)} %add_rsqrt_fusion.1, bf16[2048,768]{1,0:T(8,128)(2,1)} %all-gather.2.cloned.1.call-done, s32[128]{0:T(128)S(1)} %bitcast.20), kind=kOutput, calls=%fused_computation.21 | convolution fusion | flops 808255360 | bytes 3933696 | tf_op jit(solution)/shard_map/dot_general | solution.py:44
  65.4 0.0 copy-start.1
  65.4 0.0 copy-start.2
  65.4 1.8 convolution_bitcast_fusion
  67.2 0.0 all-reduce.2.cloned.1.call-update
  67.2 132.3 %all-reduce.2.cloned.1.call-done = f32[640,768]{1,0:T(8,128)} async-done(((f32[640,768]{1,0:T(8,128)}), f32[640,768]{1,0:T(8,128)}) %all-reduce.2.cloned.1.call-update) | async-done | bytes 1966096 | tf_op jit(solution)/shard_map/psum | solution.py:51
  199.5 0.0 copy-done.1
  199.5 0.0 copy-done.2
  199.5 1.6 multiply_subtract_fusion
  (2 shorter events, 0.0 us)
Async XLA Ops:
  7.2 31.2 %copy-start = (bf16[1,128,640]{2,1,0:T(8,128)(2,1)S(1)}, bf16[1,128,640]{2,1,0:T(8,128)(2,1)}, u32[]{:S(2)}) copy-start(bf16[1,128,640]{2,1,0:T(8,128)(2,1)} %param.8) | copy-start | bytes 491524
  7.2 53.6 %copy-start.3 = (s32[1,128]{1,0:T(1,128)S(1)}, s32[1,128]{1,0:T(1,128)}, u32[]{:S(2)}) copy-start(s32[1,128]{1,0:T(1,128)} %param.11) | copy-start | bytes 1540
  7.2 53.6 %all-gather.2.cloned.1.call-start = ((), (), s32[]{:S(2)}) async-start(), calls=%async_computation | async-start | bytes 3342336 | tf_op jit(solution)/shard_map/all_gather | solution.py:33
  10.1 189.4 %all-reduce.2.cloned.1.call-start = ((), (), s32[]{:S(2)}) async-start(), calls=%async_computation.1 | async-start | bytes 3932160 | tf_op jit(solution)/shard_map/psum | solution.py:51
  65.4 134.1 %copy-start.1 = (f32[40,768]{1,0:T(8,128)S(1)}, f32[40,768]{1,0:T(8,128)}, u32[]{:S(2)}) copy-start(f32[40,768]{1,0:T(8,128)} %param.9) | copy-start | bytes 368644
  65.4 134.1 %copy-start.2 = (f32[40,768]{1,0:T(8,128)S(1)}, f32[40,768]{1,0:T(8,128)}, u32[]{:S(2)}) copy-start(f32[40,768]{1,0:T(8,128)} %param.10) | copy-start | bytes 368644
Sparse Core Ops, SparseCore 0:
  10.3 50.3 all-gather.1
  67.3 132.1 all-reduce.1
where the time goes:
time: 208 us
  waiting for transfers between devices  153 us (74%)
  blocking collectives  27.3 us (13%)
  between operations  14.1 us (7%)
  matrix products  7.78 us (4%)
  other arithmetic  5.37 us (3%)
    psum x1, waiting for transfers between devices, per_device(): summed = lax.psum(local_term, ('dp', 'replica'))  132 us
    all_gather x1, blocking collectives, per_device(): lax.all_gather(head_low, 'dp', axis=0, tiled=True)  27.3 us
    all_gather x1, waiting for transfers between devices, per_device(): piece = lax.all_gather(image_unit, 'dp', axis=0, tiled=True)  21 us
    dot_general x1, matrix products, per_device(): jnp.dot(weights, piece, preferred_element_type=jnp.float32)  4.62 us
  transfers between devices with their start and end apart: 2, of which 2 were waited for; matrix products, arithmetic and copies ran while one was open for 1% of the time, Pallas kernels for 0%

commit v1 on v0

v1 whole, which is shorter than its diff:
```python
import jax
import jax.numpy as jnp
from jax import lax
from jax.experimental import pallas as pl
from jax.experimental.pallas import tpu as pltpu
from jax.sharding import PartitionSpec as P

logit_scale = 10.0
logit_bias = -3.0
norm_epsilon = 1e-06
momentum_decay = 0.9
blend_weight = 0.7
outer_rate = 0.7
label_bits = 6
bf16, f32 = jnp.bfloat16, jnp.float32


def local_kernel(body, outs, flops, scratch=(), **more):
    return pl.pallas_call(
        body,
        out_shape=outs,
        scratch_shapes=scratch,
        **more,
        compiler_params=pltpu.CompilerParams(vmem_limit_bytes=24 * 2**20),
        cost_estimate=pl.CostEstimate(flops=flops, bytes_accessed=2**10, transcendentals=0),
    )


def pack(feat_ref, base_ref, label_ref, head_ref, text_ref, low_ref, lane_ref, wide_ref, sems):
    pairs, k_size = feat_ref.shape
    width = base_ref.shape[1]
    copies = [
        pltpu.make_async_copy(head_ref, wide_ref, sems.at[0]),
        pltpu.make_async_copy(label_ref, lane_ref, sems.at[1]),
        pltpu.make_async_copy(feat_ref, text_ref.at[:, :k_size], sems.at[2]),
        pltpu.make_async_copy(base_ref, text_ref.at[:, k_size : k_size + width], sems.at[3]),
    ]
    for copy in copies:
        copy.start()
    copies[0].wait()
    low_ref[...] = wide_ref[...].astype(bf16)
    copies[1].wait()
    labels = jnp.broadcast_to(lane_ref[...].astype(f32), (pairs, pairs)).T.astype(jnp.int32)
    lane = lax.broadcasted_iota(jnp.int32, (pairs, pairs), 1)
    coded = jnp.where(lane < pairs // 2, labels >> label_bits, labels & (2**label_bits - 1))
    text_ref[:, k_size + width :] = coded.astype(f32).astype(bf16)
    for copy in copies[2:]:
        copy.wait()


def side_by_side(*refs):
    *parts, out_ref = refs
    for k, ref in enumerate(parts):
        out_ref[k] = ref[...]


def feature_part(own_ref, y_ref, c_ref, yc_ref, row_ref, column_ref, feat_ref, turned_ref):
    k_size = row_ref.shape[1]
    numbers = lax.broadcasted_iota(jnp.int32, (k_size, k_size), 0)
    order = (numbers == row_ref[...]).astype(f32).astype(bf16)
    numbers = lax.broadcasted_iota(jnp.int32, (k_size, k_size), 1)
    turned = (numbers == column_ref[...]).astype(f32).astype(bf16)
    feat = jnp.concatenate([ref[:, :k_size] for ref in (own_ref, y_ref, c_ref, yc_ref)])
    feat_ref[...] = jnp.dot(feat, order, preferred_element_type=f32).astype(bf16)
    turned_ref[...] = lax.dot_general(
        turned, feat, (((1,), (1,)), ((), ())), preferred_element_type=f32
    ).astype(bf16)


def text_part(own_ref, y_ref, c_ref, yc_ref, feat_ref, head_ref, unit_ref, exact_ref, inv_ref):
    k_size, width = head_ref.shape
    pairs = own_ref.shape[0]
    for part, ref in enumerate((own_ref, y_ref, c_ref, yc_ref)):
        here = slice(part * pairs, (part + 1) * pairs)
        emb = ref[:, k_size : k_size + width].astype(f32)
        emb = emb + jnp.dot(feat_ref[here, :], head_ref[...], preferred_element_type=f32)
        inv = lax.rsqrt(jnp.sum(emb * emb, axis=1, keepdims=True) + norm_epsilon)
        exact = emb * inv
        exact_ref[here, :] = exact
        unit_ref[here, :] = exact.astype(bf16)
        inv_ref[here, :] = jnp.broadcast_to(inv, (pairs, 128))


def unit_images(*refs):
    for ref, out_ref in zip(refs[: len(refs) // 2], refs[len(refs) // 2 :]):
        wide = ref[...].astype(f32)
        scale = lax.rsqrt(jnp.sum(wide * wide, axis=1, keepdims=True) + norm_epsilon)
        out_ref[...] = (wide * scale).astype(bf16)


def images_part(text_refs, unit_ref, number_ref, image_refs, out_ref, base_ref=None):
    pairs = image_refs[0].shape[0]
    code_at = text_refs[0].shape[1] - 128
    codes = jnp.concatenate([ref[:, code_at:].astype(f32) for ref in text_refs])
    targets = codes[:, :1] * 2.0**label_bits + codes[:, 64:65]
    for first in range(0, len(image_refs), 2):
        image = jnp.concatenate([ref[...] for ref in image_refs[first : first + 2]])
        here = slice(first * pairs, first * pairs + image.shape[0])
        logits = logit_scale * lax.dot_general(
            unit_ref[...], image, (((1,), (1,)), ((), ())), preferred_element_type=f32
        ) + logit_bias
        weights = jax.nn.sigmoid(logits) - (targets == number_ref[:, here]).astype(f32)
        term = jnp.dot(weights.astype(bf16), image, preferred_element_type=f32)
        if first == 0:
            out_ref[...] = term if base_ref is None else base_ref[...] + term
        else:
            out_ref[...] += term


def early_part(own_ref, y_ref, c_ref, yc_ref, unit_ref, number_ref, *refs):
    *image_refs, out_ref = refs
    images_part((own_ref, y_ref, c_ref, yc_ref), unit_ref, number_ref, image_refs, out_ref)


def late_part(own_ref, y_ref, c_ref, yc_ref, unit_ref, number_ref, early_ref, exact_ref, inv_ref, turned_ref, *refs):
    *image_refs, grad_ref, away_ref, sum_ref = refs
    images_part((own_ref, y_ref, c_ref, yc_ref), unit_ref, number_ref, image_refs, sum_ref, early_ref)
    unit_grad = logit_scale * sum_ref[...]
    exact = exact_ref[...]
    along = jnp.sum(exact * unit_grad, axis=1, keepdims=True)
    text_grad = ((unit_grad - exact * along) * inv_ref[:, :1]).astype(bf16)
    grad_ref[...] = text_grad
    half = away_ref.shape[0]
    away_ref[...] = jnp.dot(turned_ref[half:, :], text_grad, preferred_element_type=f32).astype(bf16)


def kept_part(turned_ref, grad_ref, keep_ref):
    half = keep_ref.shape[0]
    keep_ref[...] = jnp.dot(turned_ref[:half, :], grad_ref[...], preferred_element_type=f32)


def per_device(img_emb, txt_base, txt_feat, head, momentum, positive_image):
    n_dp, n_rep = lax.axis_size("dp"), lax.axis_size("replica")
    depth = n_dp // 4
    pairs, width = img_emb.shape[1:]
    rows, k_size = head.shape[0], txt_feat.shape[2]
    me, rep = lax.axis_index("dp"), lax.axis_index("replica")
    z, y, core = me // 4, (me // 2) % 2, me % 2

    def moved(array, dz=0, dy=0, dc=0, shift=0):
        perm = []
        for d in range(n_dp):
            target = d ^ (dz * 4 + dy * 2 + dc)
            for r in range(n_rep):
                perm.append((d * n_rep + r, target * n_rep + (r + shift) % n_rep))
        return lax.ppermute(array, ("dp", "replica"), perm)

    def shape(*dims, kind=bf16):
        return jax.ShapeDtypeStruct(dims, kind)

    text, low = pl.pallas_call(
        pack,
        out_shape=(shape(pairs, k_size + width + 128), shape(rows, width)),
        in_specs=[pl.BlockSpec(memory_space=pltpu.HBM)] * 4,
        scratch_shapes=[
            pltpu.VMEM((1, pairs), jnp.int32), pltpu.VMEM((rows, width), f32), pltpu.SemaphoreType.DMA((4,))
        ],
    )(txt_feat[0], txt_base[0], positive_image, head)
    text_y = moved(text, dy=1)
    line = local_kernel(side_by_side, shape(depth, rows, width), 2 * 10**10)(
        low, *[moved(low, dz=k) for k in range(1, depth)]
    )
    image_later, line = lax.optimization_barrier((img_emb[0], line))

    text_c = moved(lax.optimization_barrier((text, line))[0], dc=1)
    line_y = moved(line, dy=1)
    text_yc = moved(text_y, dc=1)
    chip = jnp.stack([line, line_y], axis=1).reshape(k_size // 2, width)
    place = lax.iota(jnp.int32, k_size)
    rel_c, rel_z, rel_y = place // (k_size // 2), (place // (rows * 2)) % depth, (place // rows) % 2
    owner = ((z ^ rel_z) * 2 + (y ^ rel_y)) * 2 + (core ^ rel_c)
    true_row = owner * rows + place % rows
    n_text = 4 * pairs
    packed = (text, text_y, text_c, text_yc)
    feats, turned = local_kernel(
        feature_part, (shape(n_text, k_size), shape(k_size, n_text)), 10 * n_text * k_size * k_size
    )(*packed, true_row[None, :], true_row[:, None])
    image = img_emb[0]
    held = {0: image}
    bit = depth // 2
    while bit > 1:
        held |= {k | bit: moved(held[k], dz=bit) for k in sorted(held)}
        bit //= 2
    held[1] = moved(image_later, dz=1)
    units = local_kernel(unit_images, [shape(pairs, width)] * len(held), 10**10)(*held.values())
    units = dict(zip(held, units))
    n_early = len(units)
    units |= {k | 1: moved(units[k], dz=1) for k in list(units) if k > 1}
    slot = jnp.array([k for k in units for _ in range(pairs)], jnp.int32)
    units = list(units.values())
    number = (((z ^ slot) * 2 + y) * 2 + core) * pairs + lax.iota(jnp.int32, depth * pairs) % pairs

    chip, feats = lax.optimization_barrier((chip, feats))
    parts = 4
    whole = [chip] + [moved(part, dc=1) for part in jnp.split(chip, parts)]
    whole = jnp.concatenate(whole)

    unit, exact, inv = local_kernel(
        text_part,
        (shape(n_text, width), shape(n_text, width, kind=f32), shape(n_text, 128, kind=f32)),
        10**6,
    )(*packed, feats, whole)
    number = number[None, :].astype(f32)
    split = n_early * pairs
    early = local_kernel(early_part, shape(n_text, width, kind=f32), 10**6)(
        *packed, unit, number[:, :split], *units[:n_early]
    )
    text_grad, away = local_kernel(
        late_part,
        (shape(n_text, width), shape(k_size // 2, width)),
        10**6,
        (pltpu.VMEM((n_text, width), f32),),
    )(*packed, unit, number[:, split:], early, exact, inv, turned, *units[n_early:])
    keep = local_kernel(kept_part, shape(k_size // 2, width, kind=f32), n_text * width * k_size)(turned, text_grad)

    kept = (keep + moved(away, dc=1).astype(f32)).reshape(depth, 2 * rows, width)
    sent = kept.astype(bf16)
    total = kept[0]
    for block in [moved(sent[k], dz=k) for k in [*range(2, depth), 1]]:
        total = total + block.astype(f32)
    sent = total.astype(bf16)
    total = lax.reduce_precision(total, 8, 7)
    terms = []
    for shift in range(1, n_rep):
        crossed = moved(sent[rows:], dy=1, shift=shift)
        terms.append(moved(sent[:rows], shift=shift).astype(f32) + crossed.astype(f32))
    terms.insert(0, total[:rows] + moved(sent[rows:], dy=1).astype(f32))
    if n_rep > 2:
        terms = [
            sum(jnp.where((rep - shift) % n_rep == owner, terms[shift], 0.0) for shift in range(n_rep))
            for owner in range(n_rep)
        ]
    grand = sum(terms[1:], terms[0])
    head_grad = grand / n_rep
    new_momentum = momentum_decay * momentum + (1.0 - momentum_decay) * head_grad
    new_head = head - outer_rate * ((1.0 - blend_weight) * head_grad + blend_weight * new_momentum)
    return (new_head, new_momentum)


def solution(mesh):
    placed = (
        P("replica", "dp", None),
        P("replica", "dp", None),
        P("replica", "dp", None),
        P("dp", None),
        P("dp", None),
        P("replica", "dp"),
    )
    return jax.shard_map(
        per_device,
        mesh=mesh,
        in_specs=placed,
        out_specs=(P("dp", None), P("dp", None)),
        check_vma=False,
    )
```

time: 208 us -> 57.5 us (0.28)
  waiting for transfers between devices: 153 us -> 23.9 us
  blocking collectives: 27.3 us -> 0 us
  starting transfers between devices: 0.08 us -> 21.3 us
  between operations: 14.1 us -> 0.88 us
  Pallas kernels: 0 us -> 7.87 us
  matrix products: 7.78 us -> 0 us
  other arithmetic: 5.37 us -> 2.2 us
    psum x1 -> x0, waiting for transfers between devices: 132 us -> none  [per_device(): summed = lax.psum(local_term, ('dp', 'replica'))]
    all_gather x1 -> x0, blocking collectives: 27.3 us -> none  [per_device(): lax.all_gather(head_low, 'dp', axis=0, tiled=True)]
    ppermute x0 -> x21, waiting for transfers between devices: none -> 23.9 us  [moved(): return lax.ppermute(array, ('dp', 'replica'), perm)]
    ppermute x0 -> x21, starting transfers between devices: none -> 21.3 us  [moved(): return lax.ppermute(array, ('dp', 'replica'), perm)]
    all_gather x1 -> x0, waiting for transfers between devices: 21 us -> none  [per_device(): piece = lax.all_gather(image_unit, 'dp', axis=0, tiled=True)]
    pallas_call x0 -> x8, Pallas kernels: none -> 7.87 us  [the longest x1 1.87 us: per_device(): pl.pallas_call(pack, out_shape=(shape(pairs, k_size + width + 128), shape...]
    dot_general x3 -> x0, matrix products: 7.78 us -> none  [the longest x1 4.62 us: per_device(): jnp.dot(weights, piece, preferred_element_type=jnp.float32)]
  transfers between devices with their start and end apart: 2 -> 21, of which waited for: 2 -> 12; matrix products, arithmetic and copies ran while one was open for 1% -> 2% of each run, Pallas kernels for 0% -> 7%
where the time goes in v1:
time: 57.5 us; the launch traced here: 57.3 us
  waiting for transfers between devices  23.9 us (42%)
  starting transfers between devices  21.3 us (37%)
  Pallas kernels  7.87 us (14%)
  other arithmetic  2.2 us (4%)
  local copies, waits for them, and re-layouts  1.04 us (2%)
  between operations  0.88 us (2%)
    ppermute x21, waiting for transfers between devices, moved(): return lax.ppermute(array, ('dp', 'replica'), perm)  23.9 us
    ppermute x21, starting transfers between devices, moved(): return lax.ppermute(array, ('dp', 'replica'), perm)  21.3 us
    pallas_call x1, Pallas kernels, per_device(): pl.pallas_call(pack, out_shape=(shape(pairs, k_size + width + 128), shape...  1.87 us
    pallas_call x1, Pallas kernels, per_device(): local_kernel(late_part, (shape(n_text, width), shape(k_size // 2, width))...  1.72 us
    pallas_call x1, Pallas kernels, per_device(): local_kernel(early_part, shape(n_text, width, kind=f32), 10 ** 6)  1.42 us
    pallas_call x1, Pallas kernels, per_device(): local_kernel(feature_part, (shape(n_text, k_size), shape(k_size, n_text))...  1.27 us
  transfers between devices with their start and end apart: 21, of which 12 were waited for; matrix products, arithmetic and copies ran while one was open for 2% of the time, Pallas kernels for 7%

profile of v1, /device:TPU:0, one launch (start us, length us, event | category | flops | bytes accessed | tf_op | source)
XLA Modules:
  0.0 57.3 jit_solution(10041460224551476816)
XLA Ops:
  0.6 1.9 %shard_map.86 = (bf16[128,1536]{1,0:T(8,128)(2,1)}, bf16[40,768]{1,0:T(8,128)(2,1)}) custom-call(bf16[128,640]{1,0:T(8,128)(2,1)} %bitcast.15, bf16[128,768]{1,0:T(8,128)(2,1)} %bitcast.14, s32[1,128]{1,0:T(1,128)} %label_ref.1, f32[40,768]{1,0:T(8,128)} %head_ref.1), custom_call_target="tpu_custom_call" | custom-call | tf_op jit(solution)/shard_map/pallas_call | solution.py:151
  2.5 5.1 %collective-permute-start.3 = (bf16[40,768]{1,0:T(8,128)(2,1)}, bf16[40,768]{1,0:T(8,128)(2,1)S(1)}, u32[]{:S(2)}, u32[]{:S(2)}) collective-permute-start(bf16[40,768]{1,0:T(8,128)(2,1)} %get-tuple-element.20.refs_0_), channel_id=1, source_target_pairs={{0,24},{1,25},{2,26},{3,27},{4,28},{5,29},{6,30},{7,31},{8,16},{9,... | collective-permute-start | bytes 184328 | tf_op jit(solution)/shard_map/ppermute | solution.py:146
  7.6 0.0 collective-permute-start.2
  7.6 0.6 %collective-permute-start.1 = (bf16[40,768]{1,0:T(8,128)(2,1)}, bf16[40,768]{1,0:T(8,128)(2,1)S(1)}, u32[]{:S(2)}, u32[]{:S(2)}) collective-permute-start(bf16[40,768]{1,0:T(8,128)(2,1)} %get-tuple-element.20.refs_0_), channel_id=1, source_target_pairs={{0,8},{1,9},{2,10},{3,11},{4,12},{5,13},{6,14},{7,15},{8,0},{9,1},... | collective-permute-start | bytes 184328 | tf_op jit(solution)/shard_map/ppermute | solution.py:146
  8.3 2.3 %collective-permute-start.11 = (bf16[128,768]{1,0:T(8,128)(2,1)}, bf16[128,768]{1,0:T(8,128)(2,1)S(1)}, u32[]{:S(2)}, u32[]{:S(2)}) collective-permute-start(bf16[128,768]{1,0:T(8,128)(2,1)} %bitcast.8), channel_id=1, source_target_pairs={{0,16},{1,17},{2,18},{3,19},{4,20},{5,21},{6,22},{7,23},{8,24},{9,... | collective-permute-start | bytes 589832 | tf_op jit(solution)/shard_map/ppermute | solution.py:146
  10.6 1.5 %collective-permute-start = (bf16[128,1536]{1,0:T(8,128)(2,1)}, bf16[128,1536]{1,0:T(8,128)(2,1)S(1)}, u32[]{:S(2)}, u32[]{:S(2)}) collective-permute-start(bf16[128,1536]{1,0:T(8,128)(2,1)} %get-tuple-element.22.own_ref), channel_id=1, source_target_pairs={{0,4},{1,5},{2,6},{3,7},{4,0},{5,1},{6,2},{7,3},{8,12},{9,13},{10,... | collective-permute-start | bytes 1179656 | tf_op jit(solution)/shard_map/ppermute | solution.py:146
  12.1 0.7 %fusion.37 = f32[512]{0:T(512)S(1)} fusion(s32[512]{0:T(512)} %constant.124.clone, s32[]{:T(128)S(6)} %select_n.152, s32[]{:T(128)S(6)} %select_n.149, s32[]{:T(128)S(6)} %select_n.145), kind=kLoop, calls=%fused_computation.83 | loop fusion | flops 7168 | bytes 4108 | tf_op jit(solution)/shard_map/convert_element_type | solution.py:203
  12.8 0.0 copy-start.1
  12.8 0.0 copy-start
  12.8 0.0 collective-permute-done.3.refs_3_
  12.8 4.1 %collective-permute-done.2.refs_2_ = bf16[40,768]{1,0:T(8,128)(2,1)S(1)} collective-permute-done((bf16[40,768]{1,0:T(8,128)(2,1)}, bf16[40,768]{1,0:T(8,128)(2,1)S(1)}, u32[]{:S(2)}, u32[]{:S(2)}) %collective-permute-start.2) | collective-permute-done | bytes 61472 | tf_op jit(solution)/shard_map/ppermute | solution.py:146
  16.9 0.0 collective-permute-done.1.refs_1_
  16.9 0.0 copy-start.2
  16.9 0.8 %copy-done.2 = bf16[40,768]{1,0:T(8,128)(2,1)S(1)} copy-done((bf16[40,768]{1,0:T(8,128)(2,1)S(1)}, bf16[40,768]{1,0:T(8,128)(2,1)}, u32[]{:S(2)}) %copy-start.2) | copy-done | bytes 61464
  17.8 0.0 copy-done.1
  17.8 0.1 collective-permute-start.12
  17.8 0.5 fusion.7.column_ref
  18.3 1.6 %collective-permute-start.6 = (bf16[4,40,768]{2,1,0:T(8,128)(2,1)S(1)}, bf16[4,40,768]{2,1,0:T(8,128)(2,1)S(1)}, u32[]{:S(2)}, u32[]{:S(2)}) collective-permute-start(bf16[4,40,768]{2,1,0:T(8,128)(2,1)S(1)} %shard_map.87), channel_id=1, source_target_pairs={{0,4},{1,5},{2,6},{3,7},{4,0},{5,1},{6,2},{7,3},{8,12},{9,13},{10,... | collective-permute-start | bytes 737288 | tf_op jit(solution)/shard_map/ppermute | solution.py:146
  19.9 0.0 copy-done
  19.9 0.0 collective-permute-start.4
  19.9 2.9 %collective-permute-done.y_ref = bf16[128,1536]{1,0:T(8,128)(2,1)S(1)} collective-permute-done((bf16[128,1536]{1,0:T(8,128)(2,1)}, bf16[128,1536]{1,0:T(8,128)(2,1)S(1)}, u32[]{:S(2)}, u32[]{:S(2)}) %collective-permute-start) | collective-permute-done | bytes 393248 | tf_op jit(solution)/shard_map/ppermute | solution.py:146
  22.8 0.0 collective-permute-start.5
  22.8 0.0 collective-permute-done.11.refs_1_
  22.8 1.5 %collective-permute-done.12.refs_2_ = bf16[128,768]{1,0:T(8,128)(2,1)S(1)} collective-permute-done((bf16[128,768]{1,0:T(8,128)(2,1)S(1)}, bf16[128,768]{1,0:T(8,128)(2,1)S(1)}, u32[]{:S(2)}, u32[]{:S(2)}) %collective-permute-start.12) | collective-permute-done | bytes 196640 | tf_op jit(solution)/shard_map/ppermute | solution.py:146
  24.4 0.2 shard_map.90
  24.6 0.6 collective-permute-start.13
  25.1 0.9 %collective-permute-done.6 = bf16[4,40,768]{2,1,0:T(8,128)(2,1)S(1)} collective-permute-done((bf16[4,40,768]{2,1,0:T(8,128)(2,1)S(1)}, bf16[4,40,768]{2,1,0:T(8,128)(2,1)S(1)}, u32[]{:S(2)}, u32[]{:S(2)}) %collective-permute-start.6) | collective-permute-done | bytes 245792 | tf_op jit(solution)/shard_map/ppermute | solution.py:146
  26.1 0.0 collective-permute-done.4.c_ref
  26.1 0.0 collective-permute-done.5.yc_ref
  26.2 1.3 %shard_map.88 = (bf16[512,640]{1,0:T(8,128)(2,1)S(1)}, bf16[640,512]{1,0:T(8,128)(2,1)S(1)}) custom-call(bf16[128,1536]{1,0:T(8,128)(2,1)S(1)} %copy-done, bf16[128,1536]{1,0:T(8,128)(2,1)S(1)} %collective-permute-done.y_ref, bf16[128,1536]{1,0:T(8,128)(2,1)S(1)} %collective-permute-done.4.c_ref, bf16[128,1536]{1,0:T(8,128)(2,1)S(1)} %collective-permute-done.5.yc_ref, ...), custom_call_target="tpu_custom_call" | custom-call | flops 2097152000 | bytes 1024 | tf_op jit(solution)/shard_map/pallas_call | solution.py:175
  27.5 0.1 collective-permute-start.8
  27.6 0.5 collective-permute-start.7
  28.1 0.1 collective-permute-start.10
  28.2 0.4 collective-permute-start.9
  28.7 0.4 collective-permute-done.7
  29.1 0.0 collective-permute-done.8
  29.1 0.6 collective-permute-done.9
  29.7 0.0 collective-permute-done.10
  29.7 1.0 %shard_map.89 = (bf16[512,768]{1,0:T(8,128)(2,1)S(1)}, f32[512,768]{1,0:T(8,128)S(1)}, f32[512,128]{1,0:T(8,128)S(1)}) custom-call(bf16[128,1536]{1,0:T(8,128)(2,1)S(1)} %copy-done, bf16[128,1536]{1,0:T(8,128)(2,1)S(1)} %collective-permute-done.y_ref, bf16[128,1536]{1,0:T(8,128)(2,1)S(1)} %collective-permute-done.4.c_ref, ...), custom_call_target="tpu_custom_call" | custom-call | flops 1000000 | bytes 1024 | tf_op jit(solution)/shard_map/pallas_call | solution.py:198
  30.7 1.4 %shard_map.91.early_ref = f32[512,768]{1,0:T(8,128)S(1)} custom-call(bf16[128,1536]{1,0:T(8,128)(2,1)S(1)} %copy-done, bf16[128,1536]{1,0:T(8,128)(2,1)S(1)} %collective-permute-done.y_ref, bf16[128,1536]{1,0:T(8,128)(2,1)S(1)} %collective-permute-done.4.c_ref, bf16[128,1536]{1,0:T(8,128)(2,1)S(1)} %collective-permute-done.5.yc_ref, ...), custom_call_target="tpu_custom_call" | custom-call | flops 1000000 | bytes 1024 | tf_op jit(solution)/shard_map/pallas_call | solution.py:205
  32.1 0.0 collective-permute-done.13.refs_0_
  32.1 1.7 %shard_map.92 = (bf16[512,768]{1,0:T(8,128)(2,1)S(1)}, bf16[320,768]{1,0:T(8,128)(2,1)S(1)}) custom-call(bf16[128,1536]{1,0:T(8,128)(2,1)S(1)} %copy-done, bf16[128,1536]{1,0:T(8,128)(2,1)S(1)} %collective-permute-done.y_ref, bf16[128,1536]{1,0:T(8,128)(2,1)S(1)} %collective-permute-done.4.c_ref, bf16[128,1536]{1,0:T(8,128)(2,1)S(1)} %collective-permute-done.5.yc_ref, ...), custom_call_target="tpu_custom_call" | custom-call | flops 1000000 | bytes 1024 | tf_op jit(solution)/shard_map/pallas_call | solution.py:208
  33.8 0.4 collective-permute-start.14
  34.2 0.4 shard_map.93
  34.7 1.1 %collective-permute-done.14 = bf16[320,768]{1,0:T(8,128)(2,1)S(1)} collective-permute-done((bf16[320,768]{1,0:T(8,128)(2,1)S(1)}, bf16[320,768]{1,0:T(8,128)(2,1)S(1)}, u32[]{:S(2)}, u32[]{:S(2)}) %collective-permute-start.14) | collective-permute-done | bytes 491552 | tf_op jit(solution)/shard_map/ppermute | solution.py:146
  35.8 0.1 fusion.43
  35.9 0.0 copy-start.3
  35.9 0.0 copy-start.4
  36.0 2.0 %collective-permute-start.15 = (bf16[80,768]{1,0:T(8,128)(2,1)S(1)}, bf16[80,768]{1,0:T(8,128)(2,1)S(1)}, u32[]{:S(2)}, u32[]{:S(2)}) collective-permute-start(bf16[80,768]{1,0:T(8,128)(2,1)S(1)} %get-tuple-element.42), channel_id=1, source_target_pairs={{0,16},{1,17},{2,18},{3,19},{4,20},{5,21},{6,22},{7,23},{8,24},{9,... | collective-permute-start | bytes 368648 | tf_op jit(solution)/shard_map/ppermute | solution.py:146
  38.0 0.1 collective-permute-start.17
  38.0 2.4 %collective-permute-start.16 = (bf16[80,768]{1,0:T(8,128)(2,1)S(1)}, bf16[80,768]{1,0:T(8,128)(2,1)S(1)}, u32[]{:S(2)}, u32[]{:S(2)}) collective-permute-start(bf16[80,768]{1,0:T(8,128)(2,1)S(1)} %get-tuple-element.44), channel_id=1, source_target_pairs={{0,24},{1,25},{2,26},{3,27},{4,28},{5,29},{6,30},{7,31},{8,16},{9,... | collective-permute-start | bytes 368648 | tf_op jit(solution)/shard_map/ppermute | solution.py:146
  40.4 5.3 %collective-permute-done.15 = bf16[80,768]{1,0:T(8,128)(2,1)S(1)} collective-permute-done((bf16[80,768]{1,0:T(8,128)(2,1)S(1)}, bf16[80,768]{1,0:T(8,128)(2,1)S(1)}, u32[]{:S(2)}, u32[]{:S(2)}) %collective-permute-start.15) | collective-permute-done | bytes 122912 | tf_op jit(solution)/shard_map/ppermute | solution.py:146
  45.7 0.0 collective-permute-done.17
  45.7 3.4 %collective-permute-done.16 = bf16[80,768]{1,0:T(8,128)(2,1)S(1)} collective-permute-done((bf16[80,768]{1,0:T(8,128)(2,1)S(1)}, bf16[80,768]{1,0:T(8,128)(2,1)S(1)}, u32[]{:S(2)}, u32[]{:S(2)}) %collective-permute-start.16) | collective-permute-done | bytes 122912 | tf_op jit(solution)/shard_map/ppermute | solution.py:146
  49.1 0.1 fusion.41
  49.2 1.6 %collective-permute-start.19 = (bf16[40,768]{1,0:T(8,128)(2,1)S(1)}, bf16[40,768]{1,0:T(8,128)(2,1)S(1)}, u32[]{:S(2)}, u32[]{:S(2)}) collective-permute-start(bf16[40,768]{1,0:T(8,128)(2,1)S(1)} %get-tuple-element.49), channel_id=1, source_target_pairs={{0,1},{1,0},{2,3},{3,2},{4,5},{5,4},{6,7},{7,6},{8,9},{9,8},{10,11... | collective-permute-start | bytes 184328 | tf_op jit(solution)/shard_map/ppermute | solution.py:146
  50.7 1.5 %collective-permute-start.20 = (bf16[40,768]{1,0:T(8,128)(2,1)S(1)}, bf16[40,768]{1,0:T(8,128)(2,1)S(1)}, u32[]{:S(2)}, u32[]{:S(2)}) collective-permute-start(bf16[40,768]{1,0:T(8,128)(2,1)S(1)} %get-tuple-element.50), channel_id=1, source_target_pairs={{0,5},{1,4},{2,7},{3,6},{4,1},{5,0},{6,3},{7,2},{8,13},{9,12},{10,... | collective-permute-start | bytes 184328 | tf_op jit(solution)/shard_map/ppermute | solution.py:146
  52.2 0.5 collective-permute-start.18
  52.7 0.7 %collective-permute-done.19 = bf16[40,768]{1,0:T(8,128)(2,1)S(1)} collective-permute-done((bf16[40,768]{1,0:T(8,128)(2,1)S(1)}, bf16[40,768]{1,0:T(8,128)(2,1)S(1)}, u32[]{:S(2)}, u32[]{:S(2)}) %collective-permute-start.19) | collective-permute-done | bytes 61472 | tf_op jit(solution)/shard_map/ppermute | solution.py:146
  53.4 2.4 %collective-permute-done.20 = bf16[40,768]{1,0:T(8,128)(2,1)S(1)} collective-permute-done((bf16[40,768]{1,0:T(8,128)(2,1)S(1)}, bf16[40,768]{1,0:T(8,128)(2,1)S(1)}, u32[]{:S(2)}, u32[]{:S(2)}) %collective-permute-start.20) | collective-permute-done | bytes 61472 | tf_op jit(solution)/shard_map/ppermute | solution.py:146
  55.8 0.7 %collective-permute-done.18 = bf16[40,768]{1,0:T(8,128)(2,1)S(1)} collective-permute-done((bf16[40,768]{1,0:T(8,128)(2,1)S(1)}, bf16[40,768]{1,0:T(8,128)(2,1)S(1)}, u32[]{:S(2)}, u32[]{:S(2)}) %collective-permute-start.18) | collective-permute-done | bytes 61472 | tf_op jit(solution)/shard_map/ppermute | solution.py:146
  56.5 0.0 copy-done.3
  56.5 0.0 copy-done.4
  56.5 0.8 %multiply_subtract_fusion = (f32[40,768]{1,0:T(8,128)}, f32[40,768]{1,0:T(8,128)}) fusion(f32[40,768]{1,0:T(8,128)S(1)} %copy-done.3, bf16[40,768]{1,0:T(8,128)(2,1)S(1)} %collective-permute-done.20, bf16[40,768]{1,0:T(8,128)(2,1)S(1)} %collective-permute-done.19, bf16[40,768]{1,0:T(8,128)(2,1)S(1)} %collective-permute-done.18, ...), kind=kLoop, calls=%fused_computation.45 | loop fusion | flops 460800 | bytes 798720 | tf_op jit(solution)/shard_map/sub | solution.py:236
  (14 shorter events, 0.3 us)
Async XLA Ops:
  2.5 10.3 %collective-permute-start.3 = (bf16[40,768]{1,0:T(8,128)(2,1)}, bf16[40,768]{1,0:T(8,128)(2,1)S(1)}, u32[]{:S(2)}, u32[]{:S(2)}) collective-permute-start(bf16[40,768]{1,0:T(8,128)(2,1)} %get-tuple-element.20.refs_0_), channel_id=1, source_target_pairs={{0,24},{1,25},{2,26},{3,27},{4,28},{5,29},{6,30},{7,31},{8,16},{9,... | collective-permute-start | bytes 184328 | tf_op jit(solution)/shard_map/ppermute | solution.py:146
  7.6 9.3 %collective-permute-start.2 = (bf16[40,768]{1,0:T(8,128)(2,1)}, bf16[40,768]{1,0:T(8,128)(2,1)S(1)}, u32[]{:S(2)}, u32[]{:S(2)}) collective-permute-start(bf16[40,768]{1,0:T(8,128)(2,1)} %get-tuple-element.20.refs_0_), channel_id=1, source_target_pairs={{0,16},{1,17},{2,18},{3,19},{4,20},{5,21},{6,22},{7,23},{8,24},{9,... | collective-permute-start | bytes 184328 | tf_op jit(solution)/shard_map/ppermute | solution.py:146
  7.6 9.3 %collective-permute-start.1 = (bf16[40,768]{1,0:T(8,128)(2,1)}, bf16[40,768]{1,0:T(8,128)(2,1)S(1)}, u32[]{:S(2)}, u32[]{:S(2)}) collective-permute-start(bf16[40,768]{1,0:T(8,128)(2,1)} %get-tuple-element.20.refs_0_), channel_id=1, source_target_pairs={{0,8},{1,9},{2,10},{3,11},{4,12},{5,13},{6,14},{7,15},{8,0},{9,1},... | collective-permute-start | bytes 184328 | tf_op jit(solution)/shard_map/ppermute | solution.py:146
  8.3 14.6 %collective-permute-start.11 = (bf16[128,768]{1,0:T(8,128)(2,1)}, bf16[128,768]{1,0:T(8,128)(2,1)S(1)}, u32[]{:S(2)}, u32[]{:S(2)}) collective-permute-start(bf16[128,768]{1,0:T(8,128)(2,1)} %bitcast.8), channel_id=1, source_target_pairs={{0,16},{1,17},{2,18},{3,19},{4,20},{5,21},{6,22},{7,23},{8,24},{9,... | collective-permute-start | bytes 589832 | tf_op jit(solution)/shard_map/ppermute | solution.py:146
  10.6 12.3 %collective-permute-start = (bf16[128,1536]{1,0:T(8,128)(2,1)}, bf16[128,1536]{1,0:T(8,128)(2,1)S(1)}, u32[]{:S(2)}, u32[]{:S(2)}) collective-permute-start(bf16[128,1536]{1,0:T(8,128)(2,1)} %get-tuple-element.22.own_ref), channel_id=1, source_target_pairs={{0,4},{1,5},{2,6},{3,7},{4,0},{5,1},{6,2},{7,3},{8,12},{9,13},{10,... | collective-permute-start | bytes 1179656 | tf_op jit(solution)/shard_map/ppermute | solution.py:146
  12.8 4.9 %copy-start.1 = (bf16[1,128,768]{2,1,0:T(8,128)(2,1)S(1)}, bf16[1,128,768]{2,1,0:T(8,128)(2,1)}, u32[]{:S(2)}) copy-start(bf16[1,128,768]{2,1,0:T(8,128)(2,1)} %param.7) | copy-start | bytes 589828
  12.8 7.1 %copy-start = (bf16[128,1536]{1,0:T(8,128)(2,1)S(1)}, bf16[128,1536]{1,0:T(8,128)(2,1)}, u32[]{:S(2)}) copy-start(bf16[128,1536]{1,0:T(8,128)(2,1)} %get-tuple-element.22.own_ref) | copy-start | bytes 1179652
  16.9 0.8 %copy-start.2 = (bf16[40,768]{1,0:T(8,128)(2,1)S(1)}, bf16[40,768]{1,0:T(8,128)(2,1)}, u32[]{:S(2)}) copy-start(bf16[40,768]{1,0:T(8,128)(2,1)} %get-tuple-element.20.refs_0_) | copy-start | bytes 184324
  17.8 6.6 %collective-permute-start.12 = (bf16[128,768]{1,0:T(8,128)(2,1)S(1)}, bf16[128,768]{1,0:T(8,128)(2,1)S(1)}, u32[]{:S(2)}, u32[]{:S(2)}) collective-permute-start(bf16[128,768]{1,0:T(8,128)(2,1)S(1)} %bitcast.9), channel_id=1, source_target_pairs={{0,8},{1,9},{2,10},{3,11},{4,12},{5,13},{6,14},{7,15},{8,0},{9,1},... | collective-permute-start | bytes 589832 | tf_op jit(solution)/shard_map/ppermute | solution.py:146
  18.3 7.7 %collective-permute-start.6 = (bf16[4,40,768]{2,1,0:T(8,128)(2,1)S(1)}, bf16[4,40,768]{2,1,0:T(8,128)(2,1)S(1)}, u32[]{:S(2)}, u32[]{:S(2)}) collective-permute-start(bf16[4,40,768]{2,1,0:T(8,128)(2,1)S(1)} %shard_map.87), channel_id=1, source_target_pairs={{0,4},{1,5},{2,6},{3,7},{4,0},{5,1},{6,2},{7,3},{8,12},{9,13},{10,... | collective-permute-start | bytes 737288 | tf_op jit(solution)/shard_map/ppermute | solution.py:146
  19.9 6.2 %collective-permute-start.4 = (bf16[128,1536]{1,0:T(8,128)(2,1)S(1)}, bf16[128,1536]{1,0:T(8,128)(2,1)S(1)}, u32[]{:S(2)}, u32[]{:S(2)}) collective-permute-start(bf16[128,1536]{1,0:T(8,128)(2,1)S(1)} %copy-done), channel_id=1, source_target_pairs={{0,2},{1,3},{2,0},{3,1},{4,6},{5,7},{6,4},{7,5},{8,10},{9,11},{10,... | collective-permute-start | bytes 1179656 | tf_op jit(solution)/shard_map/ppermute | solution.py:146
  22.8 3.3 %collective-permute-start.5 = (bf16[128,1536]{1,0:T(8,128)(2,1)S(1)}, bf16[128,1536]{1,0:T(8,128)(2,1)S(1)}, u32[]{:S(2)}, u32[]{:S(2)}) collective-permute-start(bf16[128,1536]{1,0:T(8,128)(2,1)S(1)} %collective-permute-done.y_ref), channel_id=1, source_target_pairs={{0,2},{1,3},{2,0},{3,1},{4,6},{5,7},{6,4},{7,5},{8,10},{9,11},{10,... | collective-permute-start | bytes 1179656 | tf_op jit(solution)/shard_map/ppermute | solution.py:146
  24.6 7.5 %collective-permute-start.13 = (bf16[128,768]{1,0:T(8,128)(2,1)S(1)}, bf16[128,768]{1,0:T(8,128)(2,1)S(1)}, u32[]{:S(2)}, u32[]{:S(2)}) collective-permute-start(bf16[128,768]{1,0:T(8,128)(2,1)S(1)} %get-tuple-element.30.refs_1_), channel_id=1, source_target_pairs={{0,8},{1,9},{2,10},{3,11},{4,12},{5,13},{6,14},{7,15},{8,0},{9,1},... | collective-permute-start | bytes 589832 | tf_op jit(solution)/shard_map/ppermute | solution.py:146
  27.5 1.6 %collective-permute-start.8 = (bf16[80,768]{1,0:T(8,128)(2,1)S(1)}, bf16[80,768]{1,0:T(8,128)(2,1)S(1)}, u32[]{:S(2)}, u32[]{:S(2)}) collective-permute-start(bf16[80,768]{1,0:T(8,128)(2,1)S(1)} %get-tuple-element.47), channel_id=1, source_target_pairs={{0,2},{1,3},{2,0},{3,1},{4,6},{5,7},{6,4},{7,5},{8,10},{9,11},{10,... | collective-permute-start | bytes 368648 | tf_op jit(solution)/shard_map/ppermute | solution.py:146
  27.6 1.5 %collective-permute-start.7 = (bf16[80,768]{1,0:T(8,128)(2,1)S(1)}, bf16[80,768]{1,0:T(8,128)(2,1)S(1)}, u32[]{:S(2)}, u32[]{:S(2)}) collective-permute-start(bf16[80,768]{1,0:T(8,128)(2,1)S(1)} %get-tuple-element.48), channel_id=1, source_target_pairs={{0,2},{1,3},{2,0},{3,1},{4,6},{5,7},{6,4},{7,5},{8,10},{9,11},{10,... | collective-permute-start | bytes 368648 | tf_op jit(solution)/shard_map/ppermute | solution.py:146
  28.1 1.6 %collective-permute-start.10 = (bf16[80,768]{1,0:T(8,128)(2,1)S(1)}, bf16[80,768]{1,0:T(8,128)(2,1)S(1)}, u32[]{:S(2)}, u32[]{:S(2)}) collective-permute-start(bf16[80,768]{1,0:T(8,128)(2,1)S(1)} %get-tuple-element.45), channel_id=1, source_target_pairs={{0,2},{1,3},{2,0},{3,1},{4,6},{5,7},{6,4},{7,5},{8,10},{9,11},{10,... | collective-permute-start | bytes 368648 | tf_op jit(solution)/shard_map/ppermute | solution.py:146
  28.2 1.4 %collective-permute-start.9 = (bf16[80,768]{1,0:T(8,128)(2,1)S(1)}, bf16[80,768]{1,0:T(8,128)(2,1)S(1)}, u32[]{:S(2)}, u32[]{:S(2)}) collective-permute-start(bf16[80,768]{1,0:T(8,128)(2,1)S(1)} %get-tuple-element.46), channel_id=1, source_target_pairs={{0,2},{1,3},{2,0},{3,1},{4,6},{5,7},{6,4},{7,5},{8,10},{9,11},{10,... | collective-permute-start | bytes 368648 | tf_op jit(solution)/shard_map/ppermute | solution.py:146
  33.8 1.9 %collective-permute-start.14 = (bf16[320,768]{1,0:T(8,128)(2,1)S(1)}, bf16[320,768]{1,0:T(8,128)(2,1)S(1)}, u32[]{:S(2)}, u32[]{:S(2)}) collective-permute-start(bf16[320,768]{1,0:T(8,128)(2,1)S(1)} %get-tuple-element.35), channel_id=1, source_target_pairs={{0,2},{1,3},{2,0},{3,1},{4,6},{5,7},{6,4},{7,5},{8,10},{9,11},{10,... | collective-permute-start | bytes 1474568 | tf_op jit(solution)/shard_map/ppermute | solution.py:146
  35.9 20.6 %copy-start.3 = (f32[40,768]{1,0:T(8,128)S(1)}, f32[40,768]{1,0:T(8,128)}, u32[]{:S(2)}) copy-start(f32[40,768]{1,0:T(8,128)} %head_ref.1) | copy-start | bytes 368644
  35.9 20.6 %copy-start.4 = (f32[40,768]{1,0:T(8,128)S(1)}, f32[40,768]{1,0:T(8,128)}, u32[]{:S(2)}) copy-start(f32[40,768]{1,0:T(8,128)} %param.11) | copy-start | bytes 368644
  36.0 9.7 %collective-permute-start.15 = (bf16[80,768]{1,0:T(8,128)(2,1)S(1)}, bf16[80,768]{1,0:T(8,128)(2,1)S(1)}, u32[]{:S(2)}, u32[]{:S(2)}) collective-permute-start(bf16[80,768]{1,0:T(8,128)(2,1)S(1)} %get-tuple-element.42), channel_id=1, source_target_pairs={{0,16},{1,17},{2,18},{3,19},{4,20},{5,21},{6,22},{7,23},{8,24},{9,... | collective-permute-start | bytes 368648 | tf_op jit(solution)/shard_map/ppermute | solution.py:146
  38.0 7.7 %collective-permute-start.17 = (bf16[80,768]{1,0:T(8,128)(2,1)S(1)}, bf16[80,768]{1,0:T(8,128)(2,1)S(1)}, u32[]{:S(2)}, u32[]{:S(2)}) collective-permute-start(bf16[80,768]{1,0:T(8,128)(2,1)S(1)} %get-tuple-element.43), channel_id=1, source_target_pairs={{0,8},{1,9},{2,10},{3,11},{4,12},{5,13},{6,14},{7,15},{8,0},{9,1},... | collective-permute-start | bytes 368648 | tf_op jit(solution)/shard_map/ppermute | solution.py:146
  38.0 11.0 %collective-permute-start.16 = (bf16[80,768]{1,0:T(8,128)(2,1)S(1)}, bf16[80,768]{1,0:T(8,128)(2,1)S(1)}, u32[]{:S(2)}, u32[]{:S(2)}) collective-permute-start(bf16[80,768]{1,0:T(8,128)(2,1)S(1)} %get-tuple-element.44), channel_id=1, source_target_pairs={{0,24},{1,25},{2,26},{3,27},{4,28},{5,29},{6,30},{7,31},{8,16},{9,... | collective-permute-start | bytes 368648 | tf_op jit(solution)/shard_map/ppermute | solution.py:146
  49.2 4.3 %collective-permute-start.19 = (bf16[40,768]{1,0:T(8,128)(2,1)S(1)}, bf16[40,768]{1,0:T(8,128)(2,1)S(1)}, u32[]{:S(2)}, u32[]{:S(2)}) collective-permute-start(bf16[40,768]{1,0:T(8,128)(2,1)S(1)} %get-tuple-element.49), channel_id=1, source_target_pairs={{0,1},{1,0},{2,3},{3,2},{4,5},{5,4},{6,7},{7,6},{8,9},{9,8},{10,11... | collective-permute-start | bytes 184328 | tf_op jit(solution)/shard_map/ppermute | solution.py:146
  50.7 5.1 %collective-permute-start.20 = (bf16[40,768]{1,0:T(8,128)(2,1)S(1)}, bf16[40,768]{1,0:T(8,128)(2,1)S(1)}, u32[]{:S(2)}, u32[]{:S(2)}) collective-permute-start(bf16[40,768]{1,0:T(8,128)(2,1)S(1)} %get-tuple-element.50), channel_id=1, source_target_pairs={{0,5},{1,4},{2,7},{3,6},{4,1},{5,0},{6,3},{7,2},{8,13},{9,12},{10,... | collective-permute-start | bytes 184328 | tf_op jit(solution)/shard_map/ppermute | solution.py:146
  52.2 4.3 %collective-permute-start.18 = (bf16[40,768]{1,0:T(8,128)(2,1)S(1)}, bf16[40,768]{1,0:T(8,128)(2,1)S(1)}, u32[]{:S(2)}, u32[]{:S(2)}) collective-permute-start(bf16[40,768]{1,0:T(8,128)(2,1)S(1)} %get-tuple-element.50), channel_id=1, source_target_pairs={{0,4},{1,5},{2,6},{3,7},{4,0},{5,1},{6,2},{7,3},{8,12},{9,13},{10,... | collective-permute-start | bytes 184328 | tf_op jit(solution)/shard_map/ppermute | solution.py:146

commit v2 on v1

--- a/solution.py
+++ b/solution.py
@@ -1,3 +1,5 @@
+import functools
+
 import jax
 import jax.numpy as jnp
 from jax import lax
@@ -26,25 +28,22 @@
     )
 
 
-def pack(feat_ref, base_ref, label_ref, head_ref, text_ref, low_ref, lane_ref, wide_ref, sems):
+def pack(feat_ref, base_ref, label_ref, text_ref, lane_ref, sems):
     pairs, k_size = feat_ref.shape
     width = base_ref.shape[1]
     copies = [
-        pltpu.make_async_copy(head_ref, wide_ref, sems.at[0]),
-        pltpu.make_async_copy(label_ref, lane_ref, sems.at[1]),
-        pltpu.make_async_copy(feat_ref, text_ref.at[:, :k_size], sems.at[2]),
-        pltpu.make_async_copy(base_ref, text_ref.at[:, k_size : k_size + width], sems.at[3]),
+        pltpu.make_async_copy(label_ref, lane_ref, sems.at[0]),
+        pltpu.make_async_copy(feat_ref, text_ref.at[:, :k_size], sems.at[1]),
+        pltpu.make_async_copy(base_ref, text_ref.at[:, k_size : k_size + width], sems.at[2]),
     ]
     for copy in copies:
         copy.start()
     copies[0].wait()
-    low_ref[...] = wide_ref[...].astype(bf16)
-    copies[1].wait()
     labels = jnp.broadcast_to(lane_ref[...].astype(f32), (pairs, pairs)).T.astype(jnp.int32)
     lane = lax.broadcasted_iota(jnp.int32, (pairs, pairs), 1)
     coded = jnp.where(lane < pairs // 2, labels >> label_bits, labels & (2**label_bits - 1))
     text_ref[:, k_size + width :] = coded.astype(f32).astype(bf16)
-    for copy in copies[2:]:
+    for copy in copies[1:]:
         copy.wait()
 
 
@@ -54,12 +53,13 @@
         out_ref[k] = ref[...]
 
 
-def feature_part(own_ref, y_ref, c_ref, yc_ref, row_ref, column_ref, feat_ref, turned_ref):
+def feature_part(own_ref, y_ref, c_ref, yc_ref, row_ref, feat_ref, turned_ref):
     k_size = row_ref.shape[1]
     numbers = lax.broadcasted_iota(jnp.int32, (k_size, k_size), 0)
     order = (numbers == row_ref[...]).astype(f32).astype(bf16)
     numbers = lax.broadcasted_iota(jnp.int32, (k_size, k_size), 1)
-    turned = (numbers == column_ref[...]).astype(f32).astype(bf16)
+    column = jnp.broadcast_to(row_ref[...].astype(f32), (128, k_size)).T[:, :1].astype(jnp.int32)
+    turned = (numbers == column).astype(f32).astype(bf16)
     feat = jnp.concatenate([ref[:, :k_size] for ref in (own_ref, y_ref, c_ref, yc_ref)])
     feat_ref[...] = jnp.dot(feat, order, preferred_element_type=f32).astype(bf16)
     turned_ref[...] = lax.dot_general(
@@ -88,18 +88,21 @@
         out_ref[...] = (wide * scale).astype(bf16)
 
 
-def images_part(text_refs, unit_ref, number_ref, image_refs, out_ref, base_ref=None):
+def images_part(keys, text_refs, unit_ref, me_ref, image_refs, out_ref, base_ref=None):
     pairs = image_refs[0].shape[0]
     code_at = text_refs[0].shape[1] - 128
     codes = jnp.concatenate([ref[:, code_at:].astype(f32) for ref in text_refs])
     targets = codes[:, :1] * 2.0**label_bits + codes[:, 64:65]
+    lane = lax.broadcasted_iota(jnp.int32, (1, pairs), 1)
     for first in range(0, len(image_refs), 2):
         image = jnp.concatenate([ref[...] for ref in image_refs[first : first + 2]])
-        here = slice(first * pairs, first * pairs + image.shape[0])
+        number = jnp.concatenate(
+            [(me_ref[...] ^ (4 * k)) * pairs + lane for k in keys[first : first + 2]], axis=1
+        ).astype(f32)
         logits = logit_scale * lax.dot_general(
             unit_ref[...], image, (((1,), (1,)), ((), ())), preferred_element_type=f32
         ) + logit_bias
-        weights = jax.nn.sigmoid(logits) - (targets == number_ref[:, here]).astype(f32)
+        weights = jax.nn.sigmoid(logits) - (targets == number).astype(f32)
         term = jnp.dot(weights.astype(bf16), image, preferred_element_type=f32)
         if first == 0:
             out_ref[...] = term if base_ref is None else base_ref[...] + term
@@ -107,14 +110,14 @@
             out_ref[...] += term
 
 
-def early_part(own_ref, y_ref, c_ref, yc_ref, unit_ref, number_ref, *refs):
+def early_part(keys, own_ref, y_ref, c_ref, yc_ref, unit_ref, me_ref, *refs):
     *image_refs, out_ref = refs
-    images_part((own_ref, y_ref, c_ref, yc_ref), unit_ref, number_ref, image_refs, out_ref)
-
-
-def late_part(own_ref, y_ref, c_ref, yc_ref, unit_ref, number_ref, early_ref, exact_ref, inv_ref, turned_ref, *refs):
+    images_part(keys, (own_ref, y_ref, c_ref, yc_ref), unit_ref, me_ref, image_refs, out_ref)
+
+
+def late_part(keys, own_ref, y_ref, c_ref, yc_ref, unit_ref, me_ref, early_ref, exact_ref, inv_ref, turned_ref, *refs):
     *image_refs, grad_ref, away_ref, sum_ref = refs
-    images_part((own_ref, y_ref, c_ref, yc_ref), unit_ref, number_ref, image_refs, sum_ref, early_ref)
+    images_part(keys, (own_ref, y_ref, c_ref, yc_ref), unit_ref, me_ref, image_refs, sum_ref, early_ref)
     unit_grad = logit_scale * sum_ref[...]
     exact = exact_ref[...]
     along = jnp.sum(exact * unit_grad, axis=1, keepdims=True)
@@ -148,35 +151,43 @@
     def shape(*dims, kind=bf16):
         return jax.ShapeDtypeStruct(dims, kind)
 
-    text, low = pl.pallas_call(
+    low = head.astype(bf16)
+    text = pl.pallas_call(
         pack,
-        out_shape=(shape(pairs, k_size + width + 128), shape(rows, width)),
-        in_specs=[pl.BlockSpec(memory_space=pltpu.HBM)] * 4,
-        scratch_shapes=[
-            pltpu.VMEM((1, pairs), jnp.int32), pltpu.VMEM((rows, width), f32), pltpu.SemaphoreType.DMA((4,))
-        ],
-    )(txt_feat[0], txt_base[0], positive_image, head)
+        out_shape=shape(pairs, k_size + width + 128),
+        in_specs=[pl.BlockSpec(memory_space=pltpu.HBM)] * 3,
+        scratch_shapes=[pltpu.VMEM((1, pairs), jnp.int32), pltpu.SemaphoreType.DMA((3,))],
+    )(txt_feat[0], txt_base[0], positive_image)
     text_y = moved(text, dy=1)
-    line = local_kernel(side_by_side, shape(depth, rows, width), 2 * 10**10)(
-        low, *[moved(low, dz=k) for k in range(1, depth)]
-    )
-    image_later, line = lax.optimization_barrier((img_emb[0], line))
-
-    text_c = moved(lax.optimization_barrier((text, line))[0], dc=1)
-    line_y = moved(line, dy=1)
-    text_yc = moved(text_y, dc=1)
-    chip = jnp.stack([line, line_y], axis=1).reshape(k_size // 2, width)
     place = lax.iota(jnp.int32, k_size)
     rel_c, rel_z, rel_y = place // (k_size // 2), (place // (rows * 2)) % depth, (place // rows) % 2
     owner = ((z ^ rel_z) * 2 + (y ^ rel_y)) * 2 + (core ^ rel_c)
     true_row = owner * rows + place % rows
+
+    keys, bit = [0], depth // 2
+    while bit > 1:
+        keys += [k | bit for k in sorted(keys)]
+        bit //= 2
+    keys.append(1)
+    keys += [k | 1 for k in keys if k > 1]
+    true_row = true_row[None, :]
+    me_row = jnp.full((1, pairs), me, jnp.int32)
+    line = local_kernel(side_by_side, shape(depth, rows, width), 2 * 10**10)(
+        low, *[moved(low, dz=k) for k in range(1, depth)]
+    )
+    image_later, line = lax.optimization_barrier((img_emb[0], line))
+
+    text_c = moved(lax.optimization_barrier((text, line))[0], dc=1)
+    line_y = moved(line, dy=1)
+    text_y, me_row, true_row = lax.optimization_barrier((text_y, me_row, true_row))
+    text_yc = moved(text_y, dc=1)
+    chip = jnp.stack([line, line_y], axis=1).reshape(k_size // 2, width)
     n_text = 4 * pairs
     packed = (text, text_y, text_c, text_yc)
     feats, turned = local_kernel(
         feature_part, (shape(n_text, k_size), shape(k_size, n_text)), 10 * n_text * k_size * k_size
-    )(*packed, true_row[None, :], true_row[:, None])
-    image = img_emb[0]
-    held = {0: image}
+    )(*packed, true_row)
+    held = {0: image_later}
     bit = depth // 2
     while bit > 1:
         held |= {k | bit: moved(held[k], dz=bit) for k in sorted(held)}
@@ -186,9 +197,8 @@
     units = dict(zip(held, units))
     n_early = len(units)
     units |= {k | 1: moved(units[k], dz=1) for k in list(units) if k > 1}
-    slot = jnp.array([k for k in units for _ in range(pairs)], jnp.int32)
+    assert list(units) == keys
     units = list(units.values())
-    number = (((z ^ slot) * 2 + y) * 2 + core) * pairs + lax.iota(jnp.int32, depth * pairs) % pairs
 
     chip, feats = lax.optimization_barrier((chip, feats))
     parts = 4
@@ -200,17 +210,15 @@
         (shape(n_text, width), shape(n_text, width, kind=f32), shape(n_text, 128, kind=f32)),
         10**6,
     )(*packed, feats, whole)
-    number = number[None, :].astype(f32)
-    split = n_early * pairs
-    early = local_kernel(early_part, shape(n_text, width, kind=f32), 10**6)(
-        *packed, unit, number[:, :split], *units[:n_early]
+    early = local_kernel(functools.partial(early_part, keys[:n_early]), shape(n_text, width, kind=f32), 10**6)(
+        *packed, unit, me_row, *units[:n_early]
     )
     text_grad, away = local_kernel(
-        late_part,
+        functools.partial(late_part, keys[n_early:]),
         (shape(n_text, width), shape(k_size // 2, width)),
         10**6,
         (pltpu.VMEM((n_text, width), f32),),
-    )(*packed, unit, number[:, split:], early, exact, inv, turned, *units[n_early:])
+    )(*packed, unit, me_row, early, exact, inv, turned, *units[n_early:])
     keep = local_kernel(kept_part, shape(k_size // 2, width, kind=f32), n_text * width * k_size)(turned, text_grad)
 
     kept = (keep + moved(away, dc=1).astype(f32)).reshape(depth, 2 * rows, width)

time: 57.5 us -> 56 us (0.974)
  waiting for transfers between devices: 23.9 us -> 23 us
  local copies, waits for them, and re-layouts: 1.04 us -> 0.2 us
  starting transfers between devices: 21.3 us -> 22 us
    ppermute x21, waiting for transfers between devices: 23.9 us -> 23 us  [moved(): return lax.ppermute(array, ('dp', 'replica'), perm)]
    unnamed x14 -> x12, local copies, waits for them, and re-layouts: 0.91 us -> 0.08 us
    ppermute x21, starting transfers between devices: 21.3 us -> 22 us  [moved(): return lax.ppermute(array, ('dp', 'replica'), perm)]
  transfers between devices with their start and end apart: 21 -> 21, of which waited for: 12 -> 13; matrix products, arithmetic and copies ran while one was open for 2% -> 0% of each run, Pallas kernels for 7% -> 11%
where the time goes in v2:
time: 56 us; the launch traced here: 55.6 us
  waiting for transfers between devices  23 us (41%)
  starting transfers between devices  22 us (39%)
  Pallas kernels  7.67 us (14%)
  other arithmetic  1.93 us (3%)
  between operations  0.86 us (2%)
    ppermute x21, waiting for transfers between devices, moved(): return lax.ppermute(array, ('dp', 'replica'), perm)  23 us
    ppermute x21, starting transfers between devices, moved(): return lax.ppermute(array, ('dp', 'replica'), perm)  22 us
    pallas_call x1, Pallas kernels, per_device(): pl.pallas_call(pack, out_shape=shape(pairs, k_size + width + 128), in_spe...  1.79 us
    pallas_call x1, Pallas kernels, per_device(): local_kernel(functools.partial(late_part, keys[n_early:]), (shape(n_text,...  1.62 us
    pallas_call x1, Pallas kernels, per_device(): local_kernel(functools.partial(early_part, keys[:n_early]), shape(n_text,...  1.42 us
    pallas_call x1, Pallas kernels, per_device(): local_kernel(feature_part, (shape(n_text, k_size), shape(k_size, n_text))...  1.27 us
  transfers between devices with their start and end apart: 21, of which 13 were waited for; matrix products, arithmetic and copies ran while one was open for 0% of the time, Pallas kernels for 11%

profile of v2, /device:TPU:0, one launch (start us, length us, event | category | flops | bytes accessed | tf_op | source)
XLA Modules:
  0.0 55.6 jit_solution(13088321273668127041)
XLA Ops:
  0.6 0.9 %convert_element_type.31.refs_0_ = bf16[40,768]{1,0:T(8,128)(2,1)S(1)} convert(f32[40,768]{1,0:T(8,128)} %param.9) | non-fusion elementwise | flops 30720 | bytes 184320 | tf_op jit(solution)/shard_map/convert_element_type | solution.py:154
  1.5 5.0 %collective-permute-start.3 = (bf16[40,768]{1,0:T(8,128)(2,1)S(1)}, bf16[40,768]{1,0:T(8,128)(2,1)S(1)}, u32[]{:S(2)}, u32[]{:S(2)}) collective-permute-start(bf16[40,768]{1,0:T(8,128)(2,1)S(1)} %convert_element_type.31.refs_0_), channel_id=1, source_target_pairs={{0,24},{1,25},{2,26},{3,27},{4,28},{5,29},{6,30},{7,31},{8,16},{9,... | collective-permute-start | bytes 184328 | tf_op jit(solution)/shard_map/ppermute | solution.py:149
  6.6 0.0 collective-permute-start.2
  6.6 0.6 %collective-permute-start.1 = (bf16[40,768]{1,0:T(8,128)(2,1)S(1)}, bf16[40,768]{1,0:T(8,128)(2,1)S(1)}, u32[]{:S(2)}, u32[]{:S(2)}) collective-permute-start(bf16[40,768]{1,0:T(8,128)(2,1)S(1)} %convert_element_type.31.refs_0_), channel_id=1, source_target_pairs={{0,8},{1,9},{2,10},{3,11},{4,12},{5,13},{6,14},{7,15},{8,0},{9,1},... | collective-permute-start | bytes 184328 | tf_op jit(solution)/shard_map/ppermute | solution.py:149
  7.2 1.8 %shard_map.77.own_ref = bf16[128,1536]{1,0:T(8,128)(2,1)} custom-call(bf16[128,640]{1,0:T(8,128)(2,1)} %bitcast.14, bf16[128,768]{1,0:T(8,128)(2,1)} %bitcast.13, s32[1,128]{1,0:T(1,128)} %label_ref.1), custom_call_target="tpu_custom_call" | custom-call | tf_op jit(solution)/shard_map/pallas_call | solution.py:155
  9.0 0.0 copy-start.1
  9.0 0.0 copy-start
  9.0 1.7 %collective-permute-start = (bf16[128,1536]{1,0:T(8,128)(2,1)}, bf16[128,1536]{1,0:T(8,128)(2,1)S(1)}, u32[]{:S(2)}, u32[]{:S(2)}) collective-permute-start(bf16[128,1536]{1,0:T(8,128)(2,1)} %shard_map.77.own_ref), channel_id=1, source_target_pairs={{0,4},{1,5},{2,6},{3,7},{4,0},{5,1},{6,2},{7,3},{8,12},{9,13},{10,... | collective-permute-start | bytes 1179656 | tf_op jit(solution)/shard_map/ppermute | solution.py:149
  10.8 0.0 collective-permute-done.3.refs_3_
  10.8 1.1 %collective-permute-done.2.refs_2_ = bf16[40,768]{1,0:T(8,128)(2,1)S(1)} collective-permute-done((bf16[40,768]{1,0:T(8,128)(2,1)S(1)}, bf16[40,768]{1,0:T(8,128)(2,1)S(1)}, u32[]{:S(2)}, u32[]{:S(2)}) %collective-permute-start.2) | collective-permute-done | bytes 61472 | tf_op jit(solution)/shard_map/ppermute | solution.py:149
  11.9 0.0 collective-permute-done.1.refs_1_
  11.9 0.0 copy-done.1
  11.9 1.2 %collective-permute-start.12 = (bf16[128,768]{1,0:T(8,128)(2,1)S(1)}, bf16[128,768]{1,0:T(8,128)(2,1)S(1)}, u32[]{:S(2)}, u32[]{:S(2)}) collective-permute-start(bf16[128,768]{1,0:T(8,128)(2,1)S(1)} %bitcast.7), channel_id=1, source_target_pairs={{0,8},{1,9},{2,10},{3,11},{4,12},{5,13},{6,14},{7,15},{8,0},{9,1},... | collective-permute-start | bytes 589832 | tf_op jit(solution)/shard_map/ppermute | solution.py:149
  13.1 2.2 %collective-permute-start.11 = (bf16[128,768]{1,0:T(8,128)(2,1)S(1)}, bf16[128,768]{1,0:T(8,128)(2,1)S(1)}, u32[]{:S(2)}, u32[]{:S(2)}) collective-permute-start(bf16[128,768]{1,0:T(8,128)(2,1)S(1)} %bitcast.8), channel_id=1, source_target_pairs={{0,16},{1,17},{2,18},{3,19},{4,20},{5,21},{6,22},{7,23},{8,24},{9,... | collective-permute-start | bytes 589832 | tf_op jit(solution)/shard_map/ppermute | solution.py:149
  15.3 1.6 %collective-permute-start.6 = (bf16[4,40,768]{2,1,0:T(8,128)(2,1)S(1)}, bf16[4,40,768]{2,1,0:T(8,128)(2,1)S(1)}, u32[]{:S(2)}, u32[]{:S(2)}) collective-permute-start(bf16[4,40,768]{2,1,0:T(8,128)(2,1)S(1)} %shard_map.78), channel_id=1, source_target_pairs={{0,4},{1,5},{2,6},{3,7},{4,0},{5,1},{6,2},{7,3},{8,12},{9,13},{10,... | collective-permute-start | bytes 737288 | tf_op jit(solution)/shard_map/ppermute | solution.py:149
  16.9 0.0 copy-done
  16.9 0.0 collective-permute-start.4
  16.9 4.5 %collective-permute-done.y_ref = bf16[128,1536]{1,0:T(8,128)(2,1)S(1)} collective-permute-done((bf16[128,1536]{1,0:T(8,128)(2,1)}, bf16[128,1536]{1,0:T(8,128)(2,1)S(1)}, u32[]{:S(2)}, u32[]{:S(2)}) %collective-permute-start) | collective-permute-done | bytes 393248 | tf_op jit(solution)/shard_map/ppermute | solution.py:149
  21.4 0.0 collective-permute-start.5
  21.4 0.4 collective-permute-done.12.refs_2_
  21.8 1.8 %collective-permute-done.11.refs_1_ = bf16[128,768]{1,0:T(8,128)(2,1)S(1)} collective-permute-done((bf16[128,768]{1,0:T(8,128)(2,1)S(1)}, bf16[128,768]{1,0:T(8,128)(2,1)S(1)}, u32[]{:S(2)}, u32[]{:S(2)}) %collective-permute-start.11) | collective-permute-done | bytes 196640 | tf_op jit(solution)/shard_map/ppermute | solution.py:149
  23.6 0.2 shard_map.81
  23.8 0.1 collective-permute-start.13
  23.9 1.0 %collective-permute-done.6 = bf16[4,40,768]{2,1,0:T(8,128)(2,1)S(1)} collective-permute-done((bf16[4,40,768]{2,1,0:T(8,128)(2,1)S(1)}, bf16[4,40,768]{2,1,0:T(8,128)(2,1)S(1)}, u32[]{:S(2)}, u32[]{:S(2)}) %collective-permute-start.6) | collective-permute-done | bytes 245792 | tf_op jit(solution)/shard_map/ppermute | solution.py:149
  25.0 0.0 collective-permute-done.4.c_ref
  25.0 0.0 collective-permute-done.5.yc_ref
  25.0 1.3 %shard_map.79 = (bf16[512,640]{1,0:T(8,128)(2,1)S(1)}, bf16[640,512]{1,0:T(8,128)(2,1)S(1)}) custom-call(bf16[128,1536]{1,0:T(8,128)(2,1)S(1)} %copy-done, bf16[128,1536]{1,0:T(8,128)(2,1)S(1)} %collective-permute-done.y_ref, bf16[128,1536]{1,0:T(8,128)(2,1)S(1)} %collective-permute-done.4.c_ref, bf16[128,1536]{1,0:T(8,128)(2,1)S(1)} %collective-permute-done.5.yc_ref, ...), custom_call_target="tpu_custom_call" | custom-call | flops 2097152000 | bytes 1024 | tf_op jit(solution)/shard_map/pallas_call | solution.py:187
  26.3 0.1 collective-permute-start.8
  26.4 0.5 collective-permute-start.7
  26.9 0.1 collective-permute-start.10
  27.1 0.4 collective-permute-start.9
  27.5 0.4 collective-permute-done.7
  27.9 0.0 collective-permute-done.8
  27.9 0.6 %collective-permute-done.9 = bf16[80,768]{1,0:T(8,128)(2,1)S(1)} collective-permute-done((bf16[80,768]{1,0:T(8,128)(2,1)S(1)}, bf16[80,768]{1,0:T(8,128)(2,1)S(1)}, u32[]{:S(2)}, u32[]{:S(2)}) %collective-permute-start.9) | collective-permute-done | bytes 122912 | tf_op jit(solution)/shard_map/ppermute | solution.py:149
  28.5 0.0 collective-permute-done.10
  28.5 0.9 %shard_map.80 = (bf16[512,768]{1,0:T(8,128)(2,1)S(1)}, f32[512,768]{1,0:T(8,128)S(1)}, f32[512,128]{1,0:T(8,128)S(1)}) custom-call(bf16[128,1536]{1,0:T(8,128)(2,1)S(1)} %copy-done, bf16[128,1536]{1,0:T(8,128)(2,1)S(1)} %collective-permute-done.y_ref, bf16[128,1536]{1,0:T(8,128)(2,1)S(1)} %collective-permute-done.4.c_ref, ...), custom_call_target="tpu_custom_call" | custom-call | flops 1000000 | bytes 1024 | tf_op jit(solution)/shard_map/pallas_call | solution.py:208
  29.5 1.4 %shard_map.82.early_ref = f32[512,768]{1,0:T(8,128)S(1)} custom-call(bf16[128,1536]{1,0:T(8,128)(2,1)S(1)} %copy-done, bf16[128,1536]{1,0:T(8,128)(2,1)S(1)} %collective-permute-done.y_ref, bf16[128,1536]{1,0:T(8,128)(2,1)S(1)} %collective-permute-done.4.c_ref, bf16[128,1536]{1,0:T(8,128)(2,1)S(1)} %collective-permute-done.5.yc_ref, ...), custom_call_target="tpu_custom_call" | custom-call | flops 1000000 | bytes 1024 | tf_op jit(solution)/shard_map/pallas_call | solution.py:213
  30.9 0.0 collective-permute-done.13.refs_0_
  30.9 1.6 %shard_map.83 = (bf16[512,768]{1,0:T(8,128)(2,1)S(1)}, bf16[320,768]{1,0:T(8,128)(2,1)S(1)}) custom-call(bf16[128,1536]{1,0:T(8,128)(2,1)S(1)} %copy-done, bf16[128,1536]{1,0:T(8,128)(2,1)S(1)} %collective-permute-done.y_ref, bf16[128,1536]{1,0:T(8,128)(2,1)S(1)} %collective-permute-done.4.c_ref, bf16[128,1536]{1,0:T(8,128)(2,1)S(1)} %collective-permute-done.5.yc_ref, ...), custom_call_target="tpu_custom_call" | custom-call | flops 1000000 | bytes 1024 | tf_op jit(solution)/shard_map/pallas_call | solution.py:216
  32.6 0.4 collective-permute-start.14
  33.0 0.4 shard_map.84
  33.4 1.1 %collective-permute-done.14 = bf16[320,768]{1,0:T(8,128)(2,1)S(1)} collective-permute-done((bf16[320,768]{1,0:T(8,128)(2,1)S(1)}, bf16[320,768]{1,0:T(8,128)(2,1)S(1)}, u32[]{:S(2)}, u32[]{:S(2)}) %collective-permute-start.14) | collective-permute-done | bytes 491552 | tf_op jit(solution)/shard_map/ppermute | solution.py:149
  34.5 0.1 fusion.18
  34.6 0.0 copy-start.2
  34.6 0.0 copy-start.3
  34.7 2.3 %collective-permute-start.15 = (bf16[80,768]{1,0:T(8,128)(2,1)S(1)}, bf16[80,768]{1,0:T(8,128)(2,1)S(1)}, u32[]{:S(2)}, u32[]{:S(2)}) collective-permute-start(bf16[80,768]{1,0:T(8,128)(2,1)S(1)} %get-tuple-element.44), channel_id=1, source_target_pairs={{0,16},{1,17},{2,18},{3,19},{4,20},{5,21},{6,22},{7,23},{8,24},{9,... | collective-permute-start | bytes 368648 | tf_op jit(solution)/shard_map/ppermute | solution.py:149
  37.0 1.8 %collective-permute-start.17 = (bf16[80,768]{1,0:T(8,128)(2,1)S(1)}, bf16[80,768]{1,0:T(8,128)(2,1)S(1)}, u32[]{:S(2)}, u32[]{:S(2)}) collective-permute-start(bf16[80,768]{1,0:T(8,128)(2,1)S(1)} %get-tuple-element.45), channel_id=1, source_target_pairs={{0,8},{1,9},{2,10},{3,11},{4,12},{5,13},{6,14},{7,15},{8,0},{9,1},... | collective-permute-start | bytes 368648 | tf_op jit(solution)/shard_map/ppermute | solution.py:149
  38.8 0.4 collective-permute-start.16
  39.1 5.6 %collective-permute-done.15 = bf16[80,768]{1,0:T(8,128)(2,1)S(1)} collective-permute-done((bf16[80,768]{1,0:T(8,128)(2,1)S(1)}, bf16[80,768]{1,0:T(8,128)(2,1)S(1)}, u32[]{:S(2)}, u32[]{:S(2)}) %collective-permute-start.15) | collective-permute-done | bytes 122912 | tf_op jit(solution)/shard_map/ppermute | solution.py:149
  44.7 0.0 collective-permute-done.17
  44.7 2.7 %collective-permute-done.16 = bf16[80,768]{1,0:T(8,128)(2,1)S(1)} collective-permute-done((bf16[80,768]{1,0:T(8,128)(2,1)S(1)}, bf16[80,768]{1,0:T(8,128)(2,1)S(1)}, u32[]{:S(2)}, u32[]{:S(2)}) %collective-permute-start.16) | collective-permute-done | bytes 122912 | tf_op jit(solution)/shard_map/ppermute | solution.py:149
  47.4 0.1 fusion.16
  47.5 1.6 %collective-permute-start.19 = (bf16[40,768]{1,0:T(8,128)(2,1)S(1)}, bf16[40,768]{1,0:T(8,128)(2,1)S(1)}, u32[]{:S(2)}, u32[]{:S(2)}) collective-permute-start(bf16[40,768]{1,0:T(8,128)(2,1)S(1)} %get-tuple-element.51), channel_id=1, source_target_pairs={{0,1},{1,0},{2,3},{3,2},{4,5},{5,4},{6,7},{7,6},{8,9},{9,8},{10,11... | collective-permute-start | bytes 184328 | tf_op jit(solution)/shard_map/ppermute | solution.py:149
  49.1 1.5 %collective-permute-start.20 = (bf16[40,768]{1,0:T(8,128)(2,1)S(1)}, bf16[40,768]{1,0:T(8,128)(2,1)S(1)}, u32[]{:S(2)}, u32[]{:S(2)}) collective-permute-start(bf16[40,768]{1,0:T(8,128)(2,1)S(1)} %get-tuple-element.52), channel_id=1, source_target_pairs={{0,5},{1,4},{2,7},{3,6},{4,1},{5,0},{6,3},{7,2},{8,13},{9,12},{10,... | collective-permute-start | bytes 184328 | tf_op jit(solution)/shard_map/ppermute | solution.py:149
  50.6 0.5 collective-permute-start.18
  51.1 0.7 %collective-permute-done.19 = bf16[40,768]{1,0:T(8,128)(2,1)S(1)} collective-permute-done((bf16[40,768]{1,0:T(8,128)(2,1)S(1)}, bf16[40,768]{1,0:T(8,128)(2,1)S(1)}, u32[]{:S(2)}, u32[]{:S(2)}) %collective-permute-start.19) | collective-permute-done | bytes 61472 | tf_op jit(solution)/shard_map/ppermute | solution.py:149
  51.8 2.4 %collective-permute-done.20 = bf16[40,768]{1,0:T(8,128)(2,1)S(1)} collective-permute-done((bf16[40,768]{1,0:T(8,128)(2,1)S(1)}, bf16[40,768]{1,0:T(8,128)(2,1)S(1)}, u32[]{:S(2)}, u32[]{:S(2)}) %collective-permute-start.20) | collective-permute-done | bytes 61472 | tf_op jit(solution)/shard_map/ppermute | solution.py:149
  54.2 0.7 %collective-permute-done.18 = bf16[40,768]{1,0:T(8,128)(2,1)S(1)} collective-permute-done((bf16[40,768]{1,0:T(8,128)(2,1)S(1)}, bf16[40,768]{1,0:T(8,128)(2,1)S(1)}, u32[]{:S(2)}, u32[]{:S(2)}) %collective-permute-start.18) | collective-permute-done | bytes 61472 | tf_op jit(solution)/shard_map/ppermute | solution.py:149
  54.8 0.0 copy-done.2
  54.8 0.0 copy-done.3
  54.9 0.8 %multiply_subtract_fusion = (f32[40,768]{1,0:T(8,128)}, f32[40,768]{1,0:T(8,128)}) fusion(f32[40,768]{1,0:T(8,128)S(1)} %copy-done.2, bf16[40,768]{1,0:T(8,128)(2,1)S(1)} %collective-permute-done.20, bf16[40,768]{1,0:T(8,128)(2,1)S(1)} %collective-permute-done.19, bf16[40,768]{1,0:T(8,128)(2,1)S(1)} %collective-permute-done.18, ...), kind=kLoop, calls=%fused_computation.8 | loop fusion | flops 460800 | bytes 798720 | tf_op jit(solution)/shard_map/sub | solution.py:244
  (13 shorter events, 0.3 us)
Async XLA Ops:
  1.5 9.2 %collective-permute-start.3 = (bf16[40,768]{1,0:T(8,128)(2,1)S(1)}, bf16[40,768]{1,0:T(8,128)(2,1)S(1)}, u32[]{:S(2)}, u32[]{:S(2)}) collective-permute-start(bf16[40,768]{1,0:T(8,128)(2,1)S(1)} %convert_element_type.31.refs_0_), channel_id=1, source_target_pairs={{0,24},{1,25},{2,26},{3,27},{4,28},{5,29},{6,30},{7,31},{8,16},{9,... | collective-permute-start | bytes 184328 | tf_op jit(solution)/shard_map/ppermute | solution.py:149
  6.6 5.3 %collective-permute-start.2 = (bf16[40,768]{1,0:T(8,128)(2,1)S(1)}, bf16[40,768]{1,0:T(8,128)(2,1)S(1)}, u32[]{:S(2)}, u32[]{:S(2)}) collective-permute-start(bf16[40,768]{1,0:T(8,128)(2,1)S(1)} %convert_element_type.31.refs_0_), channel_id=1, source_target_pairs={{0,16},{1,17},{2,18},{3,19},{4,20},{5,21},{6,22},{7,23},{8,24},{9,... | collective-permute-start | bytes 184328 | tf_op jit(solution)/shard_map/ppermute | solution.py:149
  6.6 5.3 %collective-permute-start.1 = (bf16[40,768]{1,0:T(8,128)(2,1)S(1)}, bf16[40,768]{1,0:T(8,128)(2,1)S(1)}, u32[]{:S(2)}, u32[]{:S(2)}) collective-permute-start(bf16[40,768]{1,0:T(8,128)(2,1)S(1)} %convert_element_type.31.refs_0_), channel_id=1, source_target_pairs={{0,8},{1,9},{2,10},{3,11},{4,12},{5,13},{6,14},{7,15},{8,0},{9,1},... | collective-permute-start | bytes 184328 | tf_op jit(solution)/shard_map/ppermute | solution.py:149
  9.0 2.9 %copy-start.1 = (bf16[1,128,768]{2,1,0:T(8,128)(2,1)S(1)}, bf16[1,128,768]{2,1,0:T(8,128)(2,1)}, u32[]{:S(2)}) copy-start(bf16[1,128,768]{2,1,0:T(8,128)(2,1)} %param.6) | copy-start | bytes 589828
  9.0 7.9 %copy-start = (bf16[128,1536]{1,0:T(8,128)(2,1)S(1)}, bf16[128,1536]{1,0:T(8,128)(2,1)}, u32[]{:S(2)}) copy-start(bf16[128,1536]{1,0:T(8,128)(2,1)} %shard_map.77.own_ref) | copy-start | bytes 1179652
  9.0 12.3 %collective-permute-start = (bf16[128,1536]{1,0:T(8,128)(2,1)}, bf16[128,1536]{1,0:T(8,128)(2,1)S(1)}, u32[]{:S(2)}, u32[]{:S(2)}) collective-permute-start(bf16[128,1536]{1,0:T(8,128)(2,1)} %shard_map.77.own_ref), channel_id=1, source_target_pairs={{0,4},{1,5},{2,6},{3,7},{4,0},{5,1},{6,2},{7,3},{8,12},{9,13},{10,... | collective-permute-start | bytes 1179656 | tf_op jit(solution)/shard_map/ppermute | solution.py:149
  11.9 9.9 %collective-permute-start.12 = (bf16[128,768]{1,0:T(8,128)(2,1)S(1)}, bf16[128,768]{1,0:T(8,128)(2,1)S(1)}, u32[]{:S(2)}, u32[]{:S(2)}) collective-permute-start(bf16[128,768]{1,0:T(8,128)(2,1)S(1)} %bitcast.7), channel_id=1, source_target_pairs={{0,8},{1,9},{2,10},{3,11},{4,12},{5,13},{6,14},{7,15},{8,0},{9,1},... | collective-permute-start | bytes 589832 | tf_op jit(solution)/shard_map/ppermute | solution.py:149
  13.1 10.5 %collective-permute-start.11 = (bf16[128,768]{1,0:T(8,128)(2,1)S(1)}, bf16[128,768]{1,0:T(8,128)(2,1)S(1)}, u32[]{:S(2)}, u32[]{:S(2)}) collective-permute-start(bf16[128,768]{1,0:T(8,128)(2,1)S(1)} %bitcast.8), channel_id=1, source_target_pairs={{0,16},{1,17},{2,18},{3,19},{4,20},{5,21},{6,22},{7,23},{8,24},{9,... | collective-permute-start | bytes 589832 | tf_op jit(solution)/shard_map/ppermute | solution.py:149
  15.3 9.6 %collective-permute-start.6 = (bf16[4,40,768]{2,1,0:T(8,128)(2,1)S(1)}, bf16[4,40,768]{2,1,0:T(8,128)(2,1)S(1)}, u32[]{:S(2)}, u32[]{:S(2)}) collective-permute-start(bf16[4,40,768]{2,1,0:T(8,128)(2,1)S(1)} %shard_map.78), channel_id=1, source_target_pairs={{0,4},{1,5},{2,6},{3,7},{4,0},{5,1},{6,2},{7,3},{8,12},{9,13},{10,... | collective-permute-start | bytes 737288 | tf_op jit(solution)/shard_map/ppermute | solution.py:149
  16.9 8.1 %collective-permute-start.4 = (bf16[128,1536]{1,0:T(8,128)(2,1)S(1)}, bf16[128,1536]{1,0:T(8,128)(2,1)S(1)}, u32[]{:S(2)}, u32[]{:S(2)}) collective-permute-start(bf16[128,1536]{1,0:T(8,128)(2,1)S(1)} %copy-done), channel_id=1, source_target_pairs={{0,2},{1,3},{2,0},{3,1},{4,6},{5,7},{6,4},{7,5},{8,10},{9,11},{10,... | collective-permute-start | bytes 1179656 | tf_op jit(solution)/shard_map/ppermute | solution.py:149
  21.4 3.6 %collective-permute-start.5 = (bf16[128,1536]{1,0:T(8,128)(2,1)S(1)}, bf16[128,1536]{1,0:T(8,128)(2,1)S(1)}, u32[]{:S(2)}, u32[]{:S(2)}) collective-permute-start(bf16[128,1536]{1,0:T(8,128)(2,1)S(1)} %collective-permute-done.y_ref), channel_id=1, source_target_pairs={{0,2},{1,3},{2,0},{3,1},{4,6},{5,7},{6,4},{7,5},{8,10},{9,11},{10,... | collective-permute-start | bytes 1179656 | tf_op jit(solution)/shard_map/ppermute | solution.py:149
  23.8 7.1 %collective-permute-start.13 = (bf16[128,768]{1,0:T(8,128)(2,1)S(1)}, bf16[128,768]{1,0:T(8,128)(2,1)S(1)}, u32[]{:S(2)}, u32[]{:S(2)}) collective-permute-start(bf16[128,768]{1,0:T(8,128)(2,1)S(1)} %get-tuple-element.32.refs_1_), channel_id=1, source_target_pairs={{0,8},{1,9},{2,10},{3,11},{4,12},{5,13},{6,14},{7,15},{8,0},{9,1},... | collective-permute-start | bytes 589832 | tf_op jit(solution)/shard_map/ppermute | solution.py:149
  26.3 1.6 %collective-permute-start.8 = (bf16[80,768]{1,0:T(8,128)(2,1)S(1)}, bf16[80,768]{1,0:T(8,128)(2,1)S(1)}, u32[]{:S(2)}, u32[]{:S(2)}) collective-permute-start(bf16[80,768]{1,0:T(8,128)(2,1)S(1)} %get-tuple-element.49), channel_id=1, source_target_pairs={{0,2},{1,3},{2,0},{3,1},{4,6},{5,7},{6,4},{7,5},{8,10},{9,11},{10,... | collective-permute-start | bytes 368648 | tf_op jit(solution)/shard_map/ppermute | solution.py:149
  26.4 1.5 %collective-permute-start.7 = (bf16[80,768]{1,0:T(8,128)(2,1)S(1)}, bf16[80,768]{1,0:T(8,128)(2,1)S(1)}, u32[]{:S(2)}, u32[]{:S(2)}) collective-permute-start(bf16[80,768]{1,0:T(8,128)(2,1)S(1)} %get-tuple-element.50), channel_id=1, source_target_pairs={{0,2},{1,3},{2,0},{3,1},{4,6},{5,7},{6,4},{7,5},{8,10},{9,11},{10,... | collective-permute-start | bytes 368648 | tf_op jit(solution)/shard_map/ppermute | solution.py:149
  26.9 1.6 %collective-permute-start.10 = (bf16[80,768]{1,0:T(8,128)(2,1)S(1)}, bf16[80,768]{1,0:T(8,128)(2,1)S(1)}, u32[]{:S(2)}, u32[]{:S(2)}) collective-permute-start(bf16[80,768]{1,0:T(8,128)(2,1)S(1)} %get-tuple-element.47), channel_id=1, source_target_pairs={{0,2},{1,3},{2,0},{3,1},{4,6},{5,7},{6,4},{7,5},{8,10},{9,11},{10,... | collective-permute-start | bytes 368648 | tf_op jit(solution)/shard_map/ppermute | solution.py:149
  27.1 1.4 %collective-permute-start.9 = (bf16[80,768]{1,0:T(8,128)(2,1)S(1)}, bf16[80,768]{1,0:T(8,128)(2,1)S(1)}, u32[]{:S(2)}, u32[]{:S(2)}) collective-permute-start(bf16[80,768]{1,0:T(8,128)(2,1)S(1)} %get-tuple-element.48), channel_id=1, source_target_pairs={{0,2},{1,3},{2,0},{3,1},{4,6},{5,7},{6,4},{7,5},{8,10},{9,11},{10,... | collective-permute-start | bytes 368648 | tf_op jit(solution)/shard_map/ppermute | solution.py:149
  32.6 1.9 %collective-permute-start.14 = (bf16[320,768]{1,0:T(8,128)(2,1)S(1)}, bf16[320,768]{1,0:T(8,128)(2,1)S(1)}, u32[]{:S(2)}, u32[]{:S(2)}) collective-permute-start(bf16[320,768]{1,0:T(8,128)(2,1)S(1)} %get-tuple-element.37), channel_id=1, source_target_pairs={{0,2},{1,3},{2,0},{3,1},{4,6},{5,7},{6,4},{7,5},{8,10},{9,11},{10,... | collective-permute-start | bytes 1474568 | tf_op jit(solution)/shard_map/ppermute | solution.py:149
  34.6 20.2 %copy-start.2 = (f32[40,768]{1,0:T(8,128)S(1)}, f32[40,768]{1,0:T(8,128)}, u32[]{:S(2)}) copy-start(f32[40,768]{1,0:T(8,128)} %param.9) | copy-start | bytes 368644
  34.6 20.2 %copy-start.3 = (f32[40,768]{1,0:T(8,128)S(1)}, f32[40,768]{1,0:T(8,128)}, u32[]{:S(2)}) copy-start(f32[40,768]{1,0:T(8,128)} %param.10) | copy-start | bytes 368644
  34.7 10.0 %collective-permute-start.15 = (bf16[80,768]{1,0:T(8,128)(2,1)S(1)}, bf16[80,768]{1,0:T(8,128)(2,1)S(1)}, u32[]{:S(2)}, u32[]{:S(2)}) collective-permute-start(bf16[80,768]{1,0:T(8,128)(2,1)S(1)} %get-tuple-element.44), channel_id=1, source_target_pairs={{0,16},{1,17},{2,18},{3,19},{4,20},{5,21},{6,22},{7,23},{8,24},{9,... | collective-permute-start | bytes 368648 | tf_op jit(solution)/shard_map/ppermute | solution.py:149
  37.0 7.7 %collective-permute-start.17 = (bf16[80,768]{1,0:T(8,128)(2,1)S(1)}, bf16[80,768]{1,0:T(8,128)(2,1)S(1)}, u32[]{:S(2)}, u32[]{:S(2)}) collective-permute-start(bf16[80,768]{1,0:T(8,128)(2,1)S(1)} %get-tuple-element.45), channel_id=1, source_target_pairs={{0,8},{1,9},{2,10},{3,11},{4,12},{5,13},{6,14},{7,15},{8,0},{9,1},... | collective-permute-start | bytes 368648 | tf_op jit(solution)/shard_map/ppermute | solution.py:149
  38.8 8.7 %collective-permute-start.16 = (bf16[80,768]{1,0:T(8,128)(2,1)S(1)}, bf16[80,768]{1,0:T(8,128)(2,1)S(1)}, u32[]{:S(2)}, u32[]{:S(2)}) collective-permute-start(bf16[80,768]{1,0:T(8,128)(2,1)S(1)} %get-tuple-element.46), channel_id=1, source_target_pairs={{0,24},{1,25},{2,26},{3,27},{4,28},{5,29},{6,30},{7,31},{8,16},{9,... | collective-permute-start | bytes 368648 | tf_op jit(solution)/shard_map/ppermute | solution.py:149
  47.5 4.3 %collective-permute-start.19 = (bf16[40,768]{1,0:T(8,128)(2,1)S(1)}, bf16[40,768]{1,0:T(8,128)(2,1)S(1)}, u32[]{:S(2)}, u32[]{:S(2)}) collective-permute-start(bf16[40,768]{1,0:T(8,128)(2,1)S(1)} %get-tuple-element.51), channel_id=1, source_target_pairs={{0,1},{1,0},{2,3},{3,2},{4,5},{5,4},{6,7},{7,6},{8,9},{9,8},{10,11... | collective-permute-start | bytes 184328 | tf_op jit(solution)/shard_map/ppermute | solution.py:149
  49.1 5.1 %collective-permute-start.20 = (bf16[40,768]{1,0:T(8,128)(2,1)S(1)}, bf16[40,768]{1,0:T(8,128)(2,1)S(1)}, u32[]{:S(2)}, u32[]{:S(2)}) collective-permute-start(bf16[40,768]{1,0:T(8,128)(2,1)S(1)} %get-tuple-element.52), channel_id=1, source_target_pairs={{0,5},{1,4},{2,7},{3,6},{4,1},{5,0},{6,3},{7,2},{8,13},{9,12},{10,... | collective-permute-start | bytes 184328 | tf_op jit(solution)/shard_map/ppermute | solution.py:149
  50.6 4.3 %collective-permute-start.18 = (bf16[40,768]{1,0:T(8,128)(2,1)S(1)}, bf16[40,768]{1,0:T(8,128)(2,1)S(1)}, u32[]{:S(2)}, u32[]{:S(2)}) collective-permute-start(bf16[40,768]{1,0:T(8,128)(2,1)S(1)} %get-tuple-element.52), channel_id=1, source_target_pairs={{0,4},{1,5},{2,6},{3,7},{4,0},{5,1},{6,2},{7,3},{8,12},{9,13},{10,... | collective-permute-start | bytes 184328 | tf_op jit(solution)/shard_map/ppermute | solution.py:149

commit v3 on v2

--- a/solution.py
+++ b/solution.py
@@ -53,17 +53,26 @@
         out_ref[k] = ref[...]
 
 
-def feature_part(own_ref, y_ref, c_ref, yc_ref, row_ref, feat_ref, turned_ref):
+def row_orders(row_ref, order_ref, other_ref):
     k_size = row_ref.shape[1]
     numbers = lax.broadcasted_iota(jnp.int32, (k_size, k_size), 0)
-    order = (numbers == row_ref[...]).astype(f32).astype(bf16)
+    order_ref[...] = (numbers == row_ref[...]).astype(f32).astype(bf16)
     numbers = lax.broadcasted_iota(jnp.int32, (k_size, k_size), 1)
     column = jnp.broadcast_to(row_ref[...].astype(f32), (128, k_size)).T[:, :1].astype(jnp.int32)
-    turned = (numbers == column).astype(f32).astype(bf16)
+    other_ref[...] = (numbers == column).astype(f32).astype(bf16)
+
+
+def feature_part(own_ref, y_ref, c_ref, yc_ref, order_ref, feat_ref):
+    k_size = order_ref.shape[0]
     feat = jnp.concatenate([ref[:, :k_size] for ref in (own_ref, y_ref, c_ref, yc_ref)])
-    feat_ref[...] = jnp.dot(feat, order, preferred_element_type=f32).astype(bf16)
+    feat_ref[...] = jnp.dot(feat, order_ref[...], preferred_element_type=f32).astype(bf16)
+
+
+def turned_part(own_ref, y_ref, c_ref, yc_ref, other_ref, turned_ref):
+    k_size = other_ref.shape[0]
+    feat = jnp.concatenate([ref[:, :k_size] for ref in (own_ref, y_ref, c_ref, yc_ref)])
     turned_ref[...] = lax.dot_general(
-        turned, feat, (((1,), (1,)), ((), ())), preferred_element_type=f32
+        other_ref[...], feat, (((1,), (1,)), ((), ())), preferred_element_type=f32
     ).astype(bf16)
 
 
@@ -180,13 +189,14 @@
     text_c = moved(lax.optimization_barrier((text, line))[0], dc=1)
     line_y = moved(line, dy=1)
     text_y, me_row, true_row = lax.optimization_barrier((text_y, me_row, true_row))
+    order, other = local_kernel(row_orders, (shape(k_size, k_size), shape(k_size, k_size)), 10**6)(true_row)
+    text_y, order = lax.optimization_barrier((text_y, order))
     text_yc = moved(text_y, dc=1)
     chip = jnp.stack([line, line_y], axis=1).reshape(k_size // 2, width)
     n_text = 4 * pairs
     packed = (text, text_y, text_c, text_yc)
-    feats, turned = local_kernel(
-        feature_part, (shape(n_text, k_size), shape(k_size, n_text)), 10 * n_text * k_size * k_size
-    )(*packed, true_row)
+    turned = local_kernel(turned_part, shape(k_size, n_text), 10**6)(*packed, other)
+    feats = local_kernel(feature_part, shape(n_text, k_size), 10 * n_text * k_size * k_size)(*packed, order)
     held = {0: image_later}
     bit = depth // 2
     while bit > 1:
@@ -201,8 +211,9 @@
     units = list(units.values())
 
     chip, feats = lax.optimization_barrier((chip, feats))
-    parts = 4
-    whole = [chip] + [moved(part, dc=1) for part in jnp.split(chip, parts)]
+    *parts, part = jnp.split(chip, 4)
+    part, turned = lax.optimization_barrier((part, turned))
+    whole = [chip] + [moved(part, dc=1) for part in [*parts, part]]
     whole = jnp.concatenate(whole)
 
     unit, exact, inv = local_kernel(

time: 56 us -> 56.3 us (level)
  Pallas kernels: 7.67 us -> 8.59 us
  waiting for transfers between devices: 23 us -> 22.3 us
    pallas_call x1 -> x3, Pallas kernels: 1.27 us -> 2.09 us  [the longest x1 0.75 us: per_device(): local_kernel(feature_part, shape(n_text, k_size), 10 * n_text * k_size *...]
    ppermute x21, waiting for transfers between devices: 23 us -> 22.3 us  [moved(): return lax.ppermute(array, ('dp', 'replica'), perm)]
  transfers between devices with their start and end apart: 21 -> 21, of which waited for: 13 -> 11; matrix products, arithmetic and copies ran while one was open for 0% -> 0% of each run, Pallas kernels for 11% -> 12%
where the time goes in v3:
time: 56.3 us; the launch traced here: 55.9 us
  waiting for transfers between devices  22.3 us (40%)
  starting transfers between devices  22 us (39%)
  Pallas kernels  8.59 us (15%)
  other arithmetic  1.93 us (3%)
  between operations  0.9 us (2%)
    ppermute x21, waiting for transfers between devices, moved(): return lax.ppermute(array, ('dp', 'replica'), perm)  22.3 us
    ppermute x21, starting transfers between devices, moved(): return lax.ppermute(array, ('dp', 'replica'), perm)  22 us
    pallas_call x1, Pallas kernels, per_device(): pl.pallas_call(pack, out_shape=shape(pairs, k_size + width + 128), in_spe...  1.79 us
    pallas_call x1, Pallas kernels, per_device(): local_kernel(functools.partial(late_part, keys[n_early:]), (shape(n_text,...  1.69 us
    pallas_call x1, Pallas kernels, per_device(): local_kernel(functools.partial(early_part, keys[:n_early]), shape(n_text,...  1.42 us
  transfers between devices with their start and end apart: 21, of which 11 were waited for; matrix products, arithmetic and copies ran while one was open for 0% of the time, Pallas kernels for 12%

profile of v3, /device:TPU:0, one launch (start us, length us, event | category | flops | bytes accessed | tf_op | source)
XLA Modules:
  0.0 55.9 jit_solution(4442645884205556001)
XLA Ops:
  0.6 0.9 %convert_element_type.31.refs_0_ = bf16[40,768]{1,0:T(8,128)(2,1)S(1)} convert(f32[40,768]{1,0:T(8,128)} %param.9) | non-fusion elementwise | flops 30720 | bytes 184320 | tf_op jit(solution)/shard_map/convert_element_type | solution.py:163
  1.5 5.0 %collective-permute-start.2 = (bf16[40,768]{1,0:T(8,128)(2,1)S(1)}, bf16[40,768]{1,0:T(8,128)(2,1)S(1)}, u32[]{:S(2)}, u32[]{:S(2)}) collective-permute-start(bf16[40,768]{1,0:T(8,128)(2,1)S(1)} %convert_element_type.31.refs_0_), channel_id=1, source_target_pairs={{0,24},{1,25},{2,26},{3,27},{4,28},{5,29},{6,30},{7,31},{8,16},{9,... | collective-permute-start | bytes 184328 | tf_op jit(solution)/shard_map/ppermute | solution.py:158
  6.6 0.0 collective-permute-start.1
  6.6 0.6 %collective-permute-start = (bf16[40,768]{1,0:T(8,128)(2,1)S(1)}, bf16[40,768]{1,0:T(8,128)(2,1)S(1)}, u32[]{:S(2)}, u32[]{:S(2)}) collective-permute-start(bf16[40,768]{1,0:T(8,128)(2,1)S(1)} %convert_element_type.31.refs_0_), channel_id=1, source_target_pairs={{0,8},{1,9},{2,10},{3,11},{4,12},{5,13},{6,14},{7,15},{8,0},{9,1},... | collective-permute-start | bytes 184328 | tf_op jit(solution)/shard_map/ppermute | solution.py:158
  7.2 1.8 %shard_map.78.own_ref = bf16[128,1536]{1,0:T(8,128)(2,1)} custom-call(bf16[128,640]{1,0:T(8,128)(2,1)} %bitcast.14, bf16[128,768]{1,0:T(8,128)(2,1)} %bitcast.13, s32[1,128]{1,0:T(1,128)} %label_ref.1), custom_call_target="tpu_custom_call" | custom-call | tf_op jit(solution)/shard_map/pallas_call | solution.py:164
  9.0 0.0 copy-start.1
  9.0 0.0 copy-start
  9.0 1.7 %collective-permute-start.4 = (bf16[128,1536]{1,0:T(8,128)(2,1)}, bf16[128,1536]{1,0:T(8,128)(2,1)S(1)}, u32[]{:S(2)}, u32[]{:S(2)}) collective-permute-start(bf16[128,1536]{1,0:T(8,128)(2,1)} %shard_map.78.own_ref), channel_id=1, source_target_pairs={{0,4},{1,5},{2,6},{3,7},{4,0},{5,1},{6,2},{7,3},{8,12},{9,13},{10,... | collective-permute-start | bytes 1179656 | tf_op jit(solution)/shard_map/ppermute | solution.py:158
  10.8 0.0 collective-permute-done.2.refs_3_
  10.8 1.1 %collective-permute-done.1.refs_2_ = bf16[40,768]{1,0:T(8,128)(2,1)S(1)} collective-permute-done((bf16[40,768]{1,0:T(8,128)(2,1)S(1)}, bf16[40,768]{1,0:T(8,128)(2,1)S(1)}, u32[]{:S(2)}, u32[]{:S(2)}) %collective-permute-start.1) | collective-permute-done | bytes 61472 | tf_op jit(solution)/shard_map/ppermute | solution.py:158
  11.9 0.0 collective-permute-done.refs_1_
  11.9 0.0 copy-done.1
  11.9 1.2 %collective-permute-start.12 = (bf16[128,768]{1,0:T(8,128)(2,1)S(1)}, bf16[128,768]{1,0:T(8,128)(2,1)S(1)}, u32[]{:S(2)}, u32[]{:S(2)}) collective-permute-start(bf16[128,768]{1,0:T(8,128)(2,1)S(1)} %bitcast.7), channel_id=1, source_target_pairs={{0,8},{1,9},{2,10},{3,11},{4,12},{5,13},{6,14},{7,15},{8,0},{9,1},... | collective-permute-start | bytes 589832 | tf_op jit(solution)/shard_map/ppermute | solution.py:158
  13.1 2.2 %collective-permute-start.11 = (bf16[128,768]{1,0:T(8,128)(2,1)S(1)}, bf16[128,768]{1,0:T(8,128)(2,1)S(1)}, u32[]{:S(2)}, u32[]{:S(2)}) collective-permute-start(bf16[128,768]{1,0:T(8,128)(2,1)S(1)} %bitcast.8), channel_id=1, source_target_pairs={{0,16},{1,17},{2,18},{3,19},{4,20},{5,21},{6,22},{7,23},{8,24},{9,... | collective-permute-start | bytes 589832 | tf_op jit(solution)/shard_map/ppermute | solution.py:158
  15.3 1.6 %collective-permute-start.3 = (bf16[4,40,768]{2,1,0:T(8,128)(2,1)S(1)}, bf16[4,40,768]{2,1,0:T(8,128)(2,1)S(1)}, u32[]{:S(2)}, u32[]{:S(2)}) collective-permute-start(bf16[4,40,768]{2,1,0:T(8,128)(2,1)S(1)} %shard_map.77), channel_id=1, source_target_pairs={{0,4},{1,5},{2,6},{3,7},{4,0},{5,1},{6,2},{7,3},{8,12},{9,13},{10,... | collective-permute-start | bytes 737288 | tf_op jit(solution)/shard_map/ppermute | solution.py:158
  16.9 0.0 copy-done
  16.9 0.0 collective-permute-start.5
  16.9 4.5 %collective-permute-done.4.y_ref = bf16[128,1536]{1,0:T(8,128)(2,1)S(1)} collective-permute-done((bf16[128,1536]{1,0:T(8,128)(2,1)}, bf16[128,1536]{1,0:T(8,128)(2,1)S(1)}, u32[]{:S(2)}, u32[]{:S(2)}) %collective-permute-start.4) | collective-permute-done | bytes 393248 | tf_op jit(solution)/shard_map/ppermute | solution.py:158
  21.4 0.6 %shard_map.79 = (bf16[640,640]{1,0:T(8,128)(2,1)S(1)}, bf16[640,640]{1,0:T(8,128)(2,1)S(1)}) custom-call(s32[1,640]{1,0:T(1,128)S(1)} %fusion.4.row_ref), custom_call_target="tpu_custom_call" | custom-call | flops 1000000 | bytes 1024 | tf_op jit(solution)/shard_map/pallas_call | solution.py:192
  22.0 0.1 collective-permute-start.6
  22.1 0.0 collective-permute-done.12.refs_2_
  22.1 1.5 %collective-permute-done.11.refs_1_ = bf16[128,768]{1,0:T(8,128)(2,1)S(1)} collective-permute-done((bf16[128,768]{1,0:T(8,128)(2,1)S(1)}, bf16[128,768]{1,0:T(8,128)(2,1)S(1)}, u32[]{:S(2)}, u32[]{:S(2)}) %collective-permute-start.11) | collective-permute-done | bytes 196640 | tf_op jit(solution)/shard_map/ppermute | solution.py:158
  23.6 0.2 shard_map.83
  23.8 0.1 collective-permute-start.13
  23.9 1.0 %collective-permute-done.3 = bf16[4,40,768]{2,1,0:T(8,128)(2,1)S(1)} collective-permute-done((bf16[4,40,768]{2,1,0:T(8,128)(2,1)S(1)}, bf16[4,40,768]{2,1,0:T(8,128)(2,1)S(1)}, u32[]{:S(2)}, u32[]{:S(2)}) %collective-permute-start.3) | collective-permute-done | bytes 245792 | tf_op jit(solution)/shard_map/ppermute | solution.py:158
  25.0 0.0 collective-permute-done.5.c_ref
  25.0 0.0 collective-permute-done.6.yc_ref
  25.0 0.7 %shard_map.80.feat_ref = bf16[512,640]{1,0:T(8,128)(2,1)S(1)} custom-call(bf16[128,1536]{1,0:T(8,128)(2,1)S(1)} %copy-done, bf16[128,1536]{1,0:T(8,128)(2,1)S(1)} %collective-permute-done.4.y_ref, bf16[128,1536]{1,0:T(8,128)(2,1)S(1)} %collective-permute-done.5.c_ref, bf16[128,1536]{1,0:T(8,128)(2,1)S(1)} %collective-permute-done.6.yc_ref, ...), custom_call_target="tpu_custom_call" | custom-call | flops 2097152000 | bytes 1024 | tf_op jit(solution)/shard_map/pallas_call | solution.py:199
  25.8 0.1 collective-permute-start.8
  25.9 0.5 collective-permute-start.7
  26.4 0.7 %shard_map.81.turned_ref = bf16[640,512]{1,0:T(8,128)(2,1)S(1)} custom-call(bf16[128,1536]{1,0:T(8,128)(2,1)S(1)} %copy-done, bf16[128,1536]{1,0:T(8,128)(2,1)S(1)} %collective-permute-done.4.y_ref, bf16[128,1536]{1,0:T(8,128)(2,1)S(1)} %collective-permute-done.5.c_ref, bf16[128,1536]{1,0:T(8,128)(2,1)S(1)} %collective-permute-done.6.yc_ref, ...), custom_call_target="tpu_custom_call" | custom-call | flops 1000000 | bytes 1024 | tf_op jit(solution)/shard_map/pallas_call | solution.py:198
  27.1 0.1 collective-permute-start.10
  27.3 0.4 collective-permute-start.9
  27.7 0.0 collective-permute-done.7
  27.7 0.0 collective-permute-done.8
  27.7 1.0 %collective-permute-done.9 = bf16[80,768]{1,0:T(8,128)(2,1)S(1)} collective-permute-done((bf16[80,768]{1,0:T(8,128)(2,1)S(1)}, bf16[80,768]{1,0:T(8,128)(2,1)S(1)}, u32[]{:S(2)}, u32[]{:S(2)}) %collective-permute-start.9) | collective-permute-done | bytes 122912 | tf_op jit(solution)/shard_map/ppermute | solution.py:158
  28.7 0.0 collective-permute-done.10
  28.7 1.0 %shard_map.82 = (bf16[512,768]{1,0:T(8,128)(2,1)S(1)}, f32[512,768]{1,0:T(8,128)S(1)}, f32[512,128]{1,0:T(8,128)S(1)}) custom-call(bf16[128,1536]{1,0:T(8,128)(2,1)S(1)} %copy-done, bf16[128,1536]{1,0:T(8,128)(2,1)S(1)} %collective-permute-done.4.y_ref, bf16[128,1536]{1,0:T(8,128)(2,1)S(1)} %collective-permute-done.5.c_ref, ...), custom_call_target="tpu_custom_call" | custom-call | flops 1000000 | bytes 1024 | tf_op jit(solution)/shard_map/pallas_call | solution.py:219
  29.7 1.4 %shard_map.84.early_ref = f32[512,768]{1,0:T(8,128)S(1)} custom-call(bf16[128,1536]{1,0:T(8,128)(2,1)S(1)} %copy-done, bf16[128,1536]{1,0:T(8,128)(2,1)S(1)} %collective-permute-done.4.y_ref, bf16[128,1536]{1,0:T(8,128)(2,1)S(1)} %collective-permute-done.5.c_ref, bf16[128,1536]{1,0:T(8,128)(2,1)S(1)} %collective-permute-done.6.yc_ref, ...), custom_call_target="tpu_custom_call" | custom-call | flops 1000000 | bytes 1024 | tf_op jit(solution)/shard_map/pallas_call | solution.py:224
  31.1 0.0 collective-permute-done.13.refs_0_
  31.2 1.7 %shard_map.85 = (bf16[512,768]{1,0:T(8,128)(2,1)S(1)}, bf16[320,768]{1,0:T(8,128)(2,1)S(1)}) custom-call(bf16[128,1536]{1,0:T(8,128)(2,1)S(1)} %copy-done, bf16[128,1536]{1,0:T(8,128)(2,1)S(1)} %collective-permute-done.4.y_ref, bf16[128,1536]{1,0:T(8,128)(2,1)S(1)} %collective-permute-done.5.c_ref, bf16[128,1536]{1,0:T(8,128)(2,1)S(1)} %collective-permute-done.6.yc_ref, ...), custom_call_target="tpu_custom_call" | custom-call | flops 1000000 | bytes 1024 | tf_op jit(solution)/shard_map/pallas_call | solution.py:227
  32.8 0.4 collective-permute-start.14
  33.2 0.4 shard_map.86
  33.7 1.1 %collective-permute-done.14 = bf16[320,768]{1,0:T(8,128)(2,1)S(1)} collective-permute-done((bf16[320,768]{1,0:T(8,128)(2,1)S(1)}, bf16[320,768]{1,0:T(8,128)(2,1)S(1)}, u32[]{:S(2)}, u32[]{:S(2)}) %collective-permute-start.14) | collective-permute-done | bytes 491552 | tf_op jit(solution)/shard_map/ppermute | solution.py:158
  34.8 0.1 fusion.18
  34.9 0.0 copy-start.2
  34.9 0.0 copy-start.3
  35.0 2.4 %collective-permute-start.15 = (bf16[80,768]{1,0:T(8,128)(2,1)S(1)}, bf16[80,768]{1,0:T(8,128)(2,1)S(1)}, u32[]{:S(2)}, u32[]{:S(2)}) collective-permute-start(bf16[80,768]{1,0:T(8,128)(2,1)S(1)} %get-tuple-element.52), channel_id=1, source_target_pairs={{0,16},{1,17},{2,18},{3,19},{4,20},{5,21},{6,22},{7,23},{8,24},{9,... | collective-permute-start | bytes 368648 | tf_op jit(solution)/shard_map/ppermute | solution.py:158
  37.3 1.7 %collective-permute-start.17 = (bf16[80,768]{1,0:T(8,128)(2,1)S(1)}, bf16[80,768]{1,0:T(8,128)(2,1)S(1)}, u32[]{:S(2)}, u32[]{:S(2)}) collective-permute-start(bf16[80,768]{1,0:T(8,128)(2,1)S(1)} %get-tuple-element.53), channel_id=1, source_target_pairs={{0,8},{1,9},{2,10},{3,11},{4,12},{5,13},{6,14},{7,15},{8,0},{9,1},... | collective-permute-start | bytes 368648 | tf_op jit(solution)/shard_map/ppermute | solution.py:158
  39.0 0.4 collective-permute-start.16
  39.4 5.6 %collective-permute-done.15 = bf16[80,768]{1,0:T(8,128)(2,1)S(1)} collective-permute-done((bf16[80,768]{1,0:T(8,128)(2,1)S(1)}, bf16[80,768]{1,0:T(8,128)(2,1)S(1)}, u32[]{:S(2)}, u32[]{:S(2)}) %collective-permute-start.15) | collective-permute-done | bytes 122912 | tf_op jit(solution)/shard_map/ppermute | solution.py:158
  45.0 0.0 collective-permute-done.17
  45.0 2.8 %collective-permute-done.16 = bf16[80,768]{1,0:T(8,128)(2,1)S(1)} collective-permute-done((bf16[80,768]{1,0:T(8,128)(2,1)S(1)}, bf16[80,768]{1,0:T(8,128)(2,1)S(1)}, u32[]{:S(2)}, u32[]{:S(2)}) %collective-permute-start.16) | collective-permute-done | bytes 122912 | tf_op jit(solution)/shard_map/ppermute | solution.py:158
  47.7 0.1 fusion.16
  47.8 1.6 %collective-permute-start.19 = (bf16[40,768]{1,0:T(8,128)(2,1)S(1)}, bf16[40,768]{1,0:T(8,128)(2,1)S(1)}, u32[]{:S(2)}, u32[]{:S(2)}) collective-permute-start(bf16[40,768]{1,0:T(8,128)(2,1)S(1)} %get-tuple-element.59), channel_id=1, source_target_pairs={{0,1},{1,0},{2,3},{3,2},{4,5},{5,4},{6,7},{7,6},{8,9},{9,8},{10,11... | collective-permute-start | bytes 184328 | tf_op jit(solution)/shard_map/ppermute | solution.py:158
  49.4 1.5 %collective-permute-start.20 = (bf16[40,768]{1,0:T(8,128)(2,1)S(1)}, bf16[40,768]{1,0:T(8,128)(2,1)S(1)}, u32[]{:S(2)}, u32[]{:S(2)}) collective-permute-start(bf16[40,768]{1,0:T(8,128)(2,1)S(1)} %get-tuple-element.60), channel_id=1, source_target_pairs={{0,5},{1,4},{2,7},{3,6},{4,1},{5,0},{6,3},{7,2},{8,13},{9,12},{10,... | collective-permute-start | bytes 184328 | tf_op jit(solution)/shard_map/ppermute | solution.py:158
  50.9 0.5 collective-permute-start.18
  51.4 0.7 %collective-permute-done.19 = bf16[40,768]{1,0:T(8,128)(2,1)S(1)} collective-permute-done((bf16[40,768]{1,0:T(8,128)(2,1)S(1)}, bf16[40,768]{1,0:T(8,128)(2,1)S(1)}, u32[]{:S(2)}, u32[]{:S(2)}) %collective-permute-start.19) | collective-permute-done | bytes 61472 | tf_op jit(solution)/shard_map/ppermute | solution.py:158
  52.1 2.4 %collective-permute-done.20 = bf16[40,768]{1,0:T(8,128)(2,1)S(1)} collective-permute-done((bf16[40,768]{1,0:T(8,128)(2,1)S(1)}, bf16[40,768]{1,0:T(8,128)(2,1)S(1)}, u32[]{:S(2)}, u32[]{:S(2)}) %collective-permute-start.20) | collective-permute-done | bytes 61472 | tf_op jit(solution)/shard_map/ppermute | solution.py:158
  54.5 0.7 %collective-permute-done.18 = bf16[40,768]{1,0:T(8,128)(2,1)S(1)} collective-permute-done((bf16[40,768]{1,0:T(8,128)(2,1)S(1)}, bf16[40,768]{1,0:T(8,128)(2,1)S(1)}, u32[]{:S(2)}, u32[]{:S(2)}) %collective-permute-start.18) | collective-permute-done | bytes 61472 | tf_op jit(solution)/shard_map/ppermute | solution.py:158
  55.1 0.0 copy-done.2
  55.2 0.0 copy-done.3
  55.2 0.8 %multiply_subtract_fusion = (f32[40,768]{1,0:T(8,128)}, f32[40,768]{1,0:T(8,128)}) fusion(f32[40,768]{1,0:T(8,128)S(1)} %copy-done.2, bf16[40,768]{1,0:T(8,128)(2,1)S(1)} %collective-permute-done.20, bf16[40,768]{1,0:T(8,128)(2,1)S(1)} %collective-permute-done.19, bf16[40,768]{1,0:T(8,128)(2,1)S(1)} %collective-permute-done.18, ...), kind=kLoop, calls=%fused_computation.8 | loop fusion | flops 460800 | bytes 798720 | tf_op jit(solution)/shard_map/sub | solution.py:255
  (13 shorter events, 0.3 us)
Async XLA Ops:
  1.5 9.2 %collective-permute-start.2 = (bf16[40,768]{1,0:T(8,128)(2,1)S(1)}, bf16[40,768]{1,0:T(8,128)(2,1)S(1)}, u32[]{:S(2)}, u32[]{:S(2)}) collective-permute-start(bf16[40,768]{1,0:T(8,128)(2,1)S(1)} %convert_element_type.31.refs_0_), channel_id=1, source_target_pairs={{0,24},{1,25},{2,26},{3,27},{4,28},{5,29},{6,30},{7,31},{8,16},{9,... | collective-permute-start | bytes 184328 | tf_op jit(solution)/shard_map/ppermute | solution.py:158
  6.6 5.3 %collective-permute-start.1 = (bf16[40,768]{1,0:T(8,128)(2,1)S(1)}, bf16[40,768]{1,0:T(8,128)(2,1)S(1)}, u32[]{:S(2)}, u32[]{:S(2)}) collective-permute-start(bf16[40,768]{1,0:T(8,128)(2,1)S(1)} %convert_element_type.31.refs_0_), channel_id=1, source_target_pairs={{0,16},{1,17},{2,18},{3,19},{4,20},{5,21},{6,22},{7,23},{8,24},{9,... | collective-permute-start | bytes 184328 | tf_op jit(solution)/shard_map/ppermute | solution.py:158
  6.6 5.3 %collective-permute-start = (bf16[40,768]{1,0:T(8,128)(2,1)S(1)}, bf16[40,768]{1,0:T(8,128)(2,1)S(1)}, u32[]{:S(2)}, u32[]{:S(2)}) collective-permute-start(bf16[40,768]{1,0:T(8,128)(2,1)S(1)} %convert_element_type.31.refs_0_), channel_id=1, source_target_pairs={{0,8},{1,9},{2,10},{3,11},{4,12},{5,13},{6,14},{7,15},{8,0},{9,1},... | collective-permute-start | bytes 184328 | tf_op jit(solution)/shard_map/ppermute | solution.py:158
  9.0 2.9 %copy-start.1 = (bf16[1,128,768]{2,1,0:T(8,128)(2,1)S(1)}, bf16[1,128,768]{2,1,0:T(8,128)(2,1)}, u32[]{:S(2)}) copy-start(bf16[1,128,768]{2,1,0:T(8,128)(2,1)} %param.6) | copy-start | bytes 589828
  9.0 7.9 %copy-start = (bf16[128,1536]{1,0:T(8,128)(2,1)S(1)}, bf16[128,1536]{1,0:T(8,128)(2,1)}, u32[]{:S(2)}) copy-start(bf16[128,1536]{1,0:T(8,128)(2,1)} %shard_map.78.own_ref) | copy-start | bytes 1179652
  9.0 12.3 %collective-permute-start.4 = (bf16[128,1536]{1,0:T(8,128)(2,1)}, bf16[128,1536]{1,0:T(8,128)(2,1)S(1)}, u32[]{:S(2)}, u32[]{:S(2)}) collective-permute-start(bf16[128,1536]{1,0:T(8,128)(2,1)} %shard_map.78.own_ref), channel_id=1, source_target_pairs={{0,4},{1,5},{2,6},{3,7},{4,0},{5,1},{6,2},{7,3},{8,12},{9,13},{10,... | collective-permute-start | bytes 1179656 | tf_op jit(solution)/shard_map/ppermute | solution.py:158
  11.9 10.2 %collective-permute-start.12 = (bf16[128,768]{1,0:T(8,128)(2,1)S(1)}, bf16[128,768]{1,0:T(8,128)(2,1)S(1)}, u32[]{:S(2)}, u32[]{:S(2)}) collective-permute-start(bf16[128,768]{1,0:T(8,128)(2,1)S(1)} %bitcast.7), channel_id=1, source_target_pairs={{0,8},{1,9},{2,10},{3,11},{4,12},{5,13},{6,14},{7,15},{8,0},{9,1},... | collective-permute-start | bytes 589832 | tf_op jit(solution)/shard_map/ppermute | solution.py:158
  13.1 10.5 %collective-permute-start.11 = (bf16[128,768]{1,0:T(8,128)(2,1)S(1)}, bf16[128,768]{1,0:T(8,128)(2,1)S(1)}, u32[]{:S(2)}, u32[]{:S(2)}) collective-permute-start(bf16[128,768]{1,0:T(8,128)(2,1)S(1)} %bitcast.8), channel_id=1, source_target_pairs={{0,16},{1,17},{2,18},{3,19},{4,20},{5,21},{6,22},{7,23},{8,24},{9,... | collective-permute-start | bytes 589832 | tf_op jit(solution)/shard_map/ppermute | solution.py:158
  15.3 9.6 %collective-permute-start.3 = (bf16[4,40,768]{2,1,0:T(8,128)(2,1)S(1)}, bf16[4,40,768]{2,1,0:T(8,128)(2,1)S(1)}, u32[]{:S(2)}, u32[]{:S(2)}) collective-permute-start(bf16[4,40,768]{2,1,0:T(8,128)(2,1)S(1)} %shard_map.77), channel_id=1, source_target_pairs={{0,4},{1,5},{2,6},{3,7},{4,0},{5,1},{6,2},{7,3},{8,12},{9,13},{10,... | collective-permute-start | bytes 737288 | tf_op jit(solution)/shard_map/ppermute | solution.py:158
  16.9 8.1 %collective-permute-start.5 = (bf16[128,1536]{1,0:T(8,128)(2,1)S(1)}, bf16[128,1536]{1,0:T(8,128)(2,1)S(1)}, u32[]{:S(2)}, u32[]{:S(2)}) collective-permute-start(bf16[128,1536]{1,0:T(8,128)(2,1)S(1)} %copy-done), channel_id=1, source_target_pairs={{0,2},{1,3},{2,0},{3,1},{4,6},{5,7},{6,4},{7,5},{8,10},{9,11},{10,... | collective-permute-start | bytes 1179656 | tf_op jit(solution)/shard_map/ppermute | solution.py:158
  22.0 3.0 %collective-permute-start.6 = (bf16[128,1536]{1,0:T(8,128)(2,1)S(1)}, bf16[128,1536]{1,0:T(8,128)(2,1)S(1)}, u32[]{:S(2)}, u32[]{:S(2)}) collective-permute-start(bf16[128,1536]{1,0:T(8,128)(2,1)S(1)} %collective-permute-done.4.y_ref), channel_id=1, source_target_pairs={{0,2},{1,3},{2,0},{3,1},{4,6},{5,7},{6,4},{7,5},{8,10},{9,11},{10,... | collective-permute-start | bytes 1179656 | tf_op jit(solution)/shard_map/ppermute | solution.py:158
  23.8 7.3 %collective-permute-start.13 = (bf16[128,768]{1,0:T(8,128)(2,1)S(1)}, bf16[128,768]{1,0:T(8,128)(2,1)S(1)}, u32[]{:S(2)}, u32[]{:S(2)}) collective-permute-start(bf16[128,768]{1,0:T(8,128)(2,1)S(1)} %get-tuple-element.40.refs_1_), channel_id=1, source_target_pairs={{0,8},{1,9},{2,10},{3,11},{4,12},{5,13},{6,14},{7,15},{8,0},{9,1},... | collective-permute-start | bytes 589832 | tf_op jit(solution)/shard_map/ppermute | solution.py:158
  25.8 1.9 %collective-permute-start.8 = (bf16[80,768]{1,0:T(8,128)(2,1)S(1)}, bf16[80,768]{1,0:T(8,128)(2,1)S(1)}, u32[]{:S(2)}, u32[]{:S(2)}) collective-permute-start(bf16[80,768]{1,0:T(8,128)(2,1)S(1)} %get-tuple-element.56), channel_id=1, source_target_pairs={{0,2},{1,3},{2,0},{3,1},{4,6},{5,7},{6,4},{7,5},{8,10},{9,11},{10,... | collective-permute-start | bytes 368648 | tf_op jit(solution)/shard_map/ppermute | solution.py:158
  25.9 1.8 %collective-permute-start.7 = (bf16[80,768]{1,0:T(8,128)(2,1)S(1)}, bf16[80,768]{1,0:T(8,128)(2,1)S(1)}, u32[]{:S(2)}, u32[]{:S(2)}) collective-permute-start(bf16[80,768]{1,0:T(8,128)(2,1)S(1)} %get-tuple-element.57), channel_id=1, source_target_pairs={{0,2},{1,3},{2,0},{3,1},{4,6},{5,7},{6,4},{7,5},{8,10},{9,11},{10,... | collective-permute-start | bytes 368648 | tf_op jit(solution)/shard_map/ppermute | solution.py:158
  27.1 1.6 %collective-permute-start.10 = (bf16[80,768]{1,0:T(8,128)(2,1)S(1)}, bf16[80,768]{1,0:T(8,128)(2,1)S(1)}, u32[]{:S(2)}, u32[]{:S(2)}) collective-permute-start(bf16[80,768]{1,0:T(8,128)(2,1)S(1)} %get-tuple-element.35), channel_id=1, source_target_pairs={{0,2},{1,3},{2,0},{3,1},{4,6},{5,7},{6,4},{7,5},{8,10},{9,11},{10,... | collective-permute-start | bytes 368648 | tf_op jit(solution)/shard_map/ppermute | solution.py:158
  27.3 1.4 %collective-permute-start.9 = (bf16[80,768]{1,0:T(8,128)(2,1)S(1)}, bf16[80,768]{1,0:T(8,128)(2,1)S(1)}, u32[]{:S(2)}, u32[]{:S(2)}) collective-permute-start(bf16[80,768]{1,0:T(8,128)(2,1)S(1)} %get-tuple-element.55), channel_id=1, source_target_pairs={{0,2},{1,3},{2,0},{3,1},{4,6},{5,7},{6,4},{7,5},{8,10},{9,11},{10,... | collective-permute-start | bytes 368648 | tf_op jit(solution)/shard_map/ppermute | solution.py:158
  32.8 1.9 %collective-permute-start.14 = (bf16[320,768]{1,0:T(8,128)(2,1)S(1)}, bf16[320,768]{1,0:T(8,128)(2,1)S(1)}, u32[]{:S(2)}, u32[]{:S(2)}) collective-permute-start(bf16[320,768]{1,0:T(8,128)(2,1)S(1)} %get-tuple-element.45), channel_id=1, source_target_pairs={{0,2},{1,3},{2,0},{3,1},{4,6},{5,7},{6,4},{7,5},{8,10},{9,11},{10,... | collective-permute-start | bytes 1474568 | tf_op jit(solution)/shard_map/ppermute | solution.py:158
  34.9 20.3 %copy-start.2 = (f32[40,768]{1,0:T(8,128)S(1)}, f32[40,768]{1,0:T(8,128)}, u32[]{:S(2)}) copy-start(f32[40,768]{1,0:T(8,128)} %param.9) | copy-start | bytes 368644
  34.9 20.2 %copy-start.3 = (f32[40,768]{1,0:T(8,128)S(1)}, f32[40,768]{1,0:T(8,128)}, u32[]{:S(2)}) copy-start(f32[40,768]{1,0:T(8,128)} %param.10) | copy-start | bytes 368644
  35.0 10.0 %collective-permute-start.15 = (bf16[80,768]{1,0:T(8,128)(2,1)S(1)}, bf16[80,768]{1,0:T(8,128)(2,1)S(1)}, u32[]{:S(2)}, u32[]{:S(2)}) collective-permute-start(bf16[80,768]{1,0:T(8,128)(2,1)S(1)} %get-tuple-element.52), channel_id=1, source_target_pairs={{0,16},{1,17},{2,18},{3,19},{4,20},{5,21},{6,22},{7,23},{8,24},{9,... | collective-permute-start | bytes 368648 | tf_op jit(solution)/shard_map/ppermute | solution.py:158
  37.3 7.7 %collective-permute-start.17 = (bf16[80,768]{1,0:T(8,128)(2,1)S(1)}, bf16[80,768]{1,0:T(8,128)(2,1)S(1)}, u32[]{:S(2)}, u32[]{:S(2)}) collective-permute-start(bf16[80,768]{1,0:T(8,128)(2,1)S(1)} %get-tuple-element.53), channel_id=1, source_target_pairs={{0,8},{1,9},{2,10},{3,11},{4,12},{5,13},{6,14},{7,15},{8,0},{9,1},... | collective-permute-start | bytes 368648 | tf_op jit(solution)/shard_map/ppermute | solution.py:158
  39.0 8.7 %collective-permute-start.16 = (bf16[80,768]{1,0:T(8,128)(2,1)S(1)}, bf16[80,768]{1,0:T(8,128)(2,1)S(1)}, u32[]{:S(2)}, u32[]{:S(2)}) collective-permute-start(bf16[80,768]{1,0:T(8,128)(2,1)S(1)} %get-tuple-element.54), channel_id=1, source_target_pairs={{0,24},{1,25},{2,26},{3,27},{4,28},{5,29},{6,30},{7,31},{8,16},{9,... | collective-permute-start | bytes 368648 | tf_op jit(solution)/shard_map/ppermute | solution.py:158
  47.8 4.3 %collective-permute-start.19 = (bf16[40,768]{1,0:T(8,128)(2,1)S(1)}, bf16[40,768]{1,0:T(8,128)(2,1)S(1)}, u32[]{:S(2)}, u32[]{:S(2)}) collective-permute-start(bf16[40,768]{1,0:T(8,128)(2,1)S(1)} %get-tuple-element.59), channel_id=1, source_target_pairs={{0,1},{1,0},{2,3},{3,2},{4,5},{5,4},{6,7},{7,6},{8,9},{9,8},{10,11... | collective-permute-start | bytes 184328 | tf_op jit(solution)/shard_map/ppermute | solution.py:158
  49.4 5.1 %collective-permute-start.20 = (bf16[40,768]{1,0:T(8,128)(2,1)S(1)}, bf16[40,768]{1,0:T(8,128)(2,1)S(1)}, u32[]{:S(2)}, u32[]{:S(2)}) collective-permute-start(bf16[40,768]{1,0:T(8,128)(2,1)S(1)} %get-tuple-element.60), channel_id=1, source_target_pairs={{0,5},{1,4},{2,7},{3,6},{4,1},{5,0},{6,3},{7,2},{8,13},{9,12},{10,... | collective-permute-start | bytes 184328 | tf_op jit(solution)/shard_map/ppermute | solution.py:158
  50.9 4.3 %collective-permute-start.18 = (bf16[40,768]{1,0:T(8,128)(2,1)S(1)}, bf16[40,768]{1,0:T(8,128)(2,1)S(1)}, u32[]{:S(2)}, u32[]{:S(2)}) collective-permute-start(bf16[40,768]{1,0:T(8,128)(2,1)S(1)} %get-tuple-element.60), channel_id=1, source_target_pairs={{0,4},{1,5},{2,6},{3,7},{4,0},{5,1},{6,2},{7,3},{8,12},{9,13},{10,... | collective-permute-start | bytes 184328 | tf_op jit(solution)/shard_map/ppermute | solution.py:158

commit v4 on v3

--- a/solution.py
+++ b/solution.py
@@ -62,15 +62,10 @@
     other_ref[...] = (numbers == column).astype(f32).astype(bf16)
 
 
-def feature_part(own_ref, y_ref, c_ref, yc_ref, order_ref, feat_ref):
+def feature_part(own_ref, y_ref, c_ref, yc_ref, order_ref, other_ref, feat_ref, turned_ref):
     k_size = order_ref.shape[0]
     feat = jnp.concatenate([ref[:, :k_size] for ref in (own_ref, y_ref, c_ref, yc_ref)])
     feat_ref[...] = jnp.dot(feat, order_ref[...], preferred_element_type=f32).astype(bf16)
-
-
-def turned_part(own_ref, y_ref, c_ref, yc_ref, other_ref, turned_ref):
-    k_size = other_ref.shape[0]
-    feat = jnp.concatenate([ref[:, :k_size] for ref in (own_ref, y_ref, c_ref, yc_ref)])
     turned_ref[...] = lax.dot_general(
         other_ref[...], feat, (((1,), (1,)), ((), ())), preferred_element_type=f32
     ).astype(bf16)
@@ -195,8 +190,9 @@
     chip = jnp.stack([line, line_y], axis=1).reshape(k_size // 2, width)
     n_text = 4 * pairs
     packed = (text, text_y, text_c, text_yc)
-    turned = local_kernel(turned_part, shape(k_size, n_text), 10**6)(*packed, other)
-    feats = local_kernel(feature_part, shape(n_text, k_size), 10 * n_text * k_size * k_size)(*packed, order)
+    feats, turned = local_kernel(
+        feature_part, (shape(n_text, k_size), shape(k_size, n_text)), 10 * n_text * k_size * k_size
+    )(*packed, order, other)
     held = {0: image_later}
     bit = depth // 2
     while bit > 1:
@@ -211,9 +207,8 @@
     units = list(units.values())
 
     chip, feats = lax.optimization_barrier((chip, feats))
-    *parts, part = jnp.split(chip, 4)
-    part, turned = lax.optimization_barrier((part, turned))
-    whole = [chip] + [moved(part, dc=1) for part in [*parts, part]]
+    parts = 4
+    whole = [chip] + [moved(part, dc=1) for part in jnp.split(chip, parts)]
     whole = jnp.concatenate(whole)
 
     unit, exact, inv = local_kernel(
@@ -235,7 +230,7 @@
     kept = (keep + moved(away, dc=1).astype(f32)).reshape(depth, 2 * rows, width)
     sent = kept.astype(bf16)
     total = kept[0]
-    for block in [moved(sent[k], dz=k) for k in [*range(2, depth), 1]]:
+    for block in [moved(sent[k], dz=k) for k in [1, *range(depth - 1, 1, -1)]]:
         total = total + block.astype(f32)
     sent = total.astype(bf16)
     total = lax.reduce_precision(total, 8, 7)

time: 56.3 us -> 56.8 us (level)
  waiting for transfers between devices: 22.3 us -> 23.3 us
    ppermute x21, waiting for transfers between devices: 22.3 us -> 23.3 us  [moved(): return lax.ppermute(array, ('dp', 'replica'), perm)]
    pallas_call x2 -> x1, Pallas kernels: 1.45 us -> 1.25 us  [per_device(): local_kernel(feature_part, (shape(n_text, k_size), shape(k_size, n_text))...]
  transfers between devices with their start and end apart: 21 -> 21, of which waited for: 11 -> 12; matrix products, arithmetic and copies ran while one was open for 0% -> 0% of each run, Pallas kernels for 12% -> 12%
where the time goes in v4:
time: 56.8 us; the launch traced here: 56.7 us
  waiting for transfers between devices  23.3 us (41%)
  starting transfers between devices  22 us (39%)
  Pallas kernels  8.28 us (15%)
  other arithmetic  1.93 us (3%)
  between operations  0.89 us (2%)
    ppermute x21, waiting for transfers between devices, moved(): return lax.ppermute(array, ('dp', 'replica'), perm)  23.3 us
    ppermute x21, starting transfers between devices, moved(): return lax.ppermute(array, ('dp', 'replica'), perm)  22 us
    pallas_call x1, Pallas kernels, per_device(): pl.pallas_call(pack, out_shape=shape(pairs, k_size + width + 128), in_spe...  1.78 us
    pallas_call x1, Pallas kernels, per_device(): local_kernel(functools.partial(late_part, keys[n_early:]), (shape(n_text,...  1.62 us
    pallas_call x1, Pallas kernels, per_device(): local_kernel(functools.partial(early_part, keys[:n_early]), shape(n_text,...  1.42 us
    pallas_call x1, Pallas kernels, per_device(): local_kernel(feature_part, (shape(n_text, k_size), shape(k_size, n_text))...  1.25 us
  transfers between devices with their start and end apart: 21, of which 12 were waited for; matrix products, arithmetic and copies ran while one was open for 0% of the time, Pallas kernels for 12%

profile of v4, /device:TPU:0, one launch (start us, length us, event | category | flops | bytes accessed | tf_op | source)
XLA Modules:
  0.0 56.7 jit_solution(17563654494239548871)
XLA Ops:
  0.6 0.9 %convert_element_type.31.refs_0_ = bf16[40,768]{1,0:T(8,128)(2,1)S(1)} convert(f32[40,768]{1,0:T(8,128)} %param.9) | non-fusion elementwise | flops 30720 | bytes 184320 | tf_op jit(solution)/shard_map/convert_element_type | solution.py:158
  1.5 5.0 %collective-permute-start.3 = (bf16[40,768]{1,0:T(8,128)(2,1)S(1)}, bf16[40,768]{1,0:T(8,128)(2,1)S(1)}, u32[]{:S(2)}, u32[]{:S(2)}) collective-permute-start(bf16[40,768]{1,0:T(8,128)(2,1)S(1)} %convert_element_type.31.refs_0_), channel_id=1, source_target_pairs={{0,24},{1,25},{2,26},{3,27},{4,28},{5,29},{6,30},{7,31},{8,16},{9,... | collective-permute-start | bytes 184328 | tf_op jit(solution)/shard_map/ppermute | solution.py:153
  6.6 0.0 collective-permute-start.2
  6.6 0.6 %collective-permute-start.1 = (bf16[40,768]{1,0:T(8,128)(2,1)S(1)}, bf16[40,768]{1,0:T(8,128)(2,1)S(1)}, u32[]{:S(2)}, u32[]{:S(2)}) collective-permute-start(bf16[40,768]{1,0:T(8,128)(2,1)S(1)} %convert_element_type.31.refs_0_), channel_id=1, source_target_pairs={{0,8},{1,9},{2,10},{3,11},{4,12},{5,13},{6,14},{7,15},{8,0},{9,1},... | collective-permute-start | bytes 184328 | tf_op jit(solution)/shard_map/ppermute | solution.py:153
  7.2 1.8 %shard_map.77.own_ref = bf16[128,1536]{1,0:T(8,128)(2,1)} custom-call(bf16[128,640]{1,0:T(8,128)(2,1)} %bitcast.14, bf16[128,768]{1,0:T(8,128)(2,1)} %bitcast.13, s32[1,128]{1,0:T(1,128)} %label_ref.1), custom_call_target="tpu_custom_call" | custom-call | tf_op jit(solution)/shard_map/pallas_call | solution.py:159
  9.0 0.0 copy-start.1
  9.0 0.0 copy-start
  9.0 1.7 %collective-permute-start = (bf16[128,1536]{1,0:T(8,128)(2,1)}, bf16[128,1536]{1,0:T(8,128)(2,1)S(1)}, u32[]{:S(2)}, u32[]{:S(2)}) collective-permute-start(bf16[128,1536]{1,0:T(8,128)(2,1)} %shard_map.77.own_ref), channel_id=1, source_target_pairs={{0,4},{1,5},{2,6},{3,7},{4,0},{5,1},{6,2},{7,3},{8,12},{9,13},{10,... | collective-permute-start | bytes 1179656 | tf_op jit(solution)/shard_map/ppermute | solution.py:153
  10.8 0.0 collective-permute-done.3.refs_3_
  10.8 1.1 %collective-permute-done.2.refs_2_ = bf16[40,768]{1,0:T(8,128)(2,1)S(1)} collective-permute-done((bf16[40,768]{1,0:T(8,128)(2,1)S(1)}, bf16[40,768]{1,0:T(8,128)(2,1)S(1)}, u32[]{:S(2)}, u32[]{:S(2)}) %collective-permute-start.2) | collective-permute-done | bytes 61472 | tf_op jit(solution)/shard_map/ppermute | solution.py:153
  11.9 0.0 collective-permute-done.1.refs_1_
  11.9 0.0 copy-done.1
  11.9 1.2 %collective-permute-start.12 = (bf16[128,768]{1,0:T(8,128)(2,1)S(1)}, bf16[128,768]{1,0:T(8,128)(2,1)S(1)}, u32[]{:S(2)}, u32[]{:S(2)}) collective-permute-start(bf16[128,768]{1,0:T(8,128)(2,1)S(1)} %bitcast.7), channel_id=1, source_target_pairs={{0,8},{1,9},{2,10},{3,11},{4,12},{5,13},{6,14},{7,15},{8,0},{9,1},... | collective-permute-start | bytes 589832 | tf_op jit(solution)/shard_map/ppermute | solution.py:153
  13.1 2.2 %collective-permute-start.11 = (bf16[128,768]{1,0:T(8,128)(2,1)S(1)}, bf16[128,768]{1,0:T(8,128)(2,1)S(1)}, u32[]{:S(2)}, u32[]{:S(2)}) collective-permute-start(bf16[128,768]{1,0:T(8,128)(2,1)S(1)} %bitcast.8), channel_id=1, source_target_pairs={{0,16},{1,17},{2,18},{3,19},{4,20},{5,21},{6,22},{7,23},{8,24},{9,... | collective-permute-start | bytes 589832 | tf_op jit(solution)/shard_map/ppermute | solution.py:153
  15.3 1.6 %collective-permute-start.6 = (bf16[4,40,768]{2,1,0:T(8,128)(2,1)S(1)}, bf16[4,40,768]{2,1,0:T(8,128)(2,1)S(1)}, u32[]{:S(2)}, u32[]{:S(2)}) collective-permute-start(bf16[4,40,768]{2,1,0:T(8,128)(2,1)S(1)} %shard_map.79), channel_id=1, source_target_pairs={{0,4},{1,5},{2,6},{3,7},{4,0},{5,1},{6,2},{7,3},{8,12},{9,13},{10,... | collective-permute-start | bytes 737288 | tf_op jit(solution)/shard_map/ppermute | solution.py:153
  16.9 0.0 copy-done
  16.9 0.0 collective-permute-start.4
  16.9 4.5 %collective-permute-done.y_ref = bf16[128,1536]{1,0:T(8,128)(2,1)S(1)} collective-permute-done((bf16[128,1536]{1,0:T(8,128)(2,1)}, bf16[128,1536]{1,0:T(8,128)(2,1)S(1)}, u32[]{:S(2)}, u32[]{:S(2)}) %collective-permute-start) | collective-permute-done | bytes 393248 | tf_op jit(solution)/shard_map/ppermute | solution.py:153
  21.4 0.6 %shard_map.78 = (bf16[640,640]{1,0:T(8,128)(2,1)S(1)}, bf16[640,640]{1,0:T(8,128)(2,1)S(1)}) custom-call(s32[1,640]{1,0:T(1,128)S(1)} %fusion.4.row_ref), custom_call_target="tpu_custom_call" | custom-call | flops 1000000 | bytes 1024 | tf_op jit(solution)/shard_map/pallas_call | solution.py:187
  22.0 0.1 collective-permute-start.5
  22.1 0.0 collective-permute-done.12.refs_2_
  22.1 1.5 %collective-permute-done.11.refs_1_ = bf16[128,768]{1,0:T(8,128)(2,1)S(1)} collective-permute-done((bf16[128,768]{1,0:T(8,128)(2,1)S(1)}, bf16[128,768]{1,0:T(8,128)(2,1)S(1)}, u32[]{:S(2)}, u32[]{:S(2)}) %collective-permute-start.11) | collective-permute-done | bytes 196640 | tf_op jit(solution)/shard_map/ppermute | solution.py:153
  23.6 0.2 shard_map.82
  23.8 0.1 collective-permute-start.13
  23.9 1.0 %collective-permute-done.6 = bf16[4,40,768]{2,1,0:T(8,128)(2,1)S(1)} collective-permute-done((bf16[4,40,768]{2,1,0:T(8,128)(2,1)S(1)}, bf16[4,40,768]{2,1,0:T(8,128)(2,1)S(1)}, u32[]{:S(2)}, u32[]{:S(2)}) %collective-permute-start.6) | collective-permute-done | bytes 245792 | tf_op jit(solution)/shard_map/ppermute | solution.py:153
  25.0 0.0 collective-permute-done.4.c_ref
  25.0 0.0 collective-permute-done.5.yc_ref
  25.0 1.3 %shard_map.80 = (bf16[512,640]{1,0:T(8,128)(2,1)S(1)}, bf16[640,512]{1,0:T(8,128)(2,1)S(1)}) custom-call(bf16[128,1536]{1,0:T(8,128)(2,1)S(1)} %copy-done, bf16[128,1536]{1,0:T(8,128)(2,1)S(1)} %collective-permute-done.y_ref, bf16[128,1536]{1,0:T(8,128)(2,1)S(1)} %collective-permute-done.4.c_ref, bf16[128,1536]{1,0:T(8,128)(2,1)S(1)} %collective-permute-done.5.yc_ref, ...), custom_call_target="tpu_custom_call" | custom-call | flops 2097152000 | bytes 1024 | tf_op jit(solution)/shard_map/pallas_call | solution.py:193
  26.3 0.1 collective-permute-start.8
  26.4 0.5 collective-permute-start.7
  26.9 0.1 collective-permute-start.10
  27.1 0.4 collective-permute-start.9
  27.5 0.4 collective-permute-done.7
  27.9 0.0 collective-permute-done.8
  27.9 0.6 %collective-permute-done.9 = bf16[80,768]{1,0:T(8,128)(2,1)S(1)} collective-permute-done((bf16[80,768]{1,0:T(8,128)(2,1)S(1)}, bf16[80,768]{1,0:T(8,128)(2,1)S(1)}, u32[]{:S(2)}, u32[]{:S(2)}) %collective-permute-start.9) | collective-permute-done | bytes 122912 | tf_op jit(solution)/shard_map/ppermute | solution.py:153
  28.5 0.0 collective-permute-done.10
  28.5 0.9 %shard_map.81 = (bf16[512,768]{1,0:T(8,128)(2,1)S(1)}, f32[512,768]{1,0:T(8,128)S(1)}, f32[512,128]{1,0:T(8,128)S(1)}) custom-call(bf16[128,1536]{1,0:T(8,128)(2,1)S(1)} %copy-done, bf16[128,1536]{1,0:T(8,128)(2,1)S(1)} %collective-permute-done.y_ref, bf16[128,1536]{1,0:T(8,128)(2,1)S(1)} %collective-permute-done.4.c_ref, ...), custom_call_target="tpu_custom_call" | custom-call | flops 1000000 | bytes 1024 | tf_op jit(solution)/shard_map/pallas_call | solution.py:214
  29.5 1.4 %shard_map.83.early_ref = f32[512,768]{1,0:T(8,128)S(1)} custom-call(bf16[128,1536]{1,0:T(8,128)(2,1)S(1)} %copy-done, bf16[128,1536]{1,0:T(8,128)(2,1)S(1)} %collective-permute-done.y_ref, bf16[128,1536]{1,0:T(8,128)(2,1)S(1)} %collective-permute-done.4.c_ref, bf16[128,1536]{1,0:T(8,128)(2,1)S(1)} %collective-permute-done.5.yc_ref, ...), custom_call_target="tpu_custom_call" | custom-call | flops 1000000 | bytes 1024 | tf_op jit(solution)/shard_map/pallas_call | solution.py:219
  30.9 0.0 collective-permute-done.13.refs_0_
  30.9 1.6 %shard_map.84 = (bf16[512,768]{1,0:T(8,128)(2,1)S(1)}, bf16[320,768]{1,0:T(8,128)(2,1)S(1)}) custom-call(bf16[128,1536]{1,0:T(8,128)(2,1)S(1)} %copy-done, bf16[128,1536]{1,0:T(8,128)(2,1)S(1)} %collective-permute-done.y_ref, bf16[128,1536]{1,0:T(8,128)(2,1)S(1)} %collective-permute-done.4.c_ref, bf16[128,1536]{1,0:T(8,128)(2,1)S(1)} %collective-permute-done.5.yc_ref, ...), custom_call_target="tpu_custom_call" | custom-call | flops 1000000 | bytes 1024 | tf_op jit(solution)/shard_map/pallas_call | solution.py:222
  32.5 0.4 collective-permute-start.14
  32.9 0.4 shard_map.85
  33.4 1.1 %collective-permute-done.14 = bf16[320,768]{1,0:T(8,128)(2,1)S(1)} collective-permute-done((bf16[320,768]{1,0:T(8,128)(2,1)S(1)}, bf16[320,768]{1,0:T(8,128)(2,1)S(1)}, u32[]{:S(2)}, u32[]{:S(2)}) %collective-permute-start.14) | collective-permute-done | bytes 491552 | tf_op jit(solution)/shard_map/ppermute | solution.py:153
  34.5 0.1 fusion.18
  34.6 0.0 copy-start.2
  34.6 0.0 copy-start.3
  34.6 1.5 %collective-permute-start.15 = (bf16[80,768]{1,0:T(8,128)(2,1)S(1)}, bf16[80,768]{1,0:T(8,128)(2,1)S(1)}, u32[]{:S(2)}, u32[]{:S(2)}) collective-permute-start(bf16[80,768]{1,0:T(8,128)(2,1)S(1)} %get-tuple-element.52), channel_id=1, source_target_pairs={{0,8},{1,9},{2,10},{3,11},{4,12},{5,13},{6,14},{7,15},{8,0},{9,1},... | collective-permute-start | bytes 368648 | tf_op jit(solution)/shard_map/ppermute | solution.py:153
  36.1 2.6 %collective-permute-start.17 = (bf16[80,768]{1,0:T(8,128)(2,1)S(1)}, bf16[80,768]{1,0:T(8,128)(2,1)S(1)}, u32[]{:S(2)}, u32[]{:S(2)}) collective-permute-start(bf16[80,768]{1,0:T(8,128)(2,1)S(1)} %get-tuple-element.53), channel_id=1, source_target_pairs={{0,16},{1,17},{2,18},{3,19},{4,20},{5,21},{6,22},{7,23},{8,24},{9,... | collective-permute-start | bytes 368648 | tf_op jit(solution)/shard_map/ppermute | solution.py:153
  38.7 0.4 collective-permute-start.16
  39.1 3.1 %collective-permute-done.15 = bf16[80,768]{1,0:T(8,128)(2,1)S(1)} collective-permute-done((bf16[80,768]{1,0:T(8,128)(2,1)S(1)}, bf16[80,768]{1,0:T(8,128)(2,1)S(1)}, u32[]{:S(2)}, u32[]{:S(2)}) %collective-permute-start.15) | collective-permute-done | bytes 122912 | tf_op jit(solution)/shard_map/ppermute | solution.py:153
  42.2 6.3 %collective-permute-done.17 = bf16[80,768]{1,0:T(8,128)(2,1)S(1)} collective-permute-done((bf16[80,768]{1,0:T(8,128)(2,1)S(1)}, bf16[80,768]{1,0:T(8,128)(2,1)S(1)}, u32[]{:S(2)}, u32[]{:S(2)}) %collective-permute-start.17) | collective-permute-done | bytes 122912 | tf_op jit(solution)/shard_map/ppermute | solution.py:153
  48.5 0.0 collective-permute-done.16
  48.5 0.1 fusion.16
  48.6 1.6 %collective-permute-start.19 = (bf16[40,768]{1,0:T(8,128)(2,1)S(1)}, bf16[40,768]{1,0:T(8,128)(2,1)S(1)}, u32[]{:S(2)}, u32[]{:S(2)}) collective-permute-start(bf16[40,768]{1,0:T(8,128)(2,1)S(1)} %get-tuple-element.59), channel_id=1, source_target_pairs={{0,1},{1,0},{2,3},{3,2},{4,5},{5,4},{6,7},{7,6},{8,9},{9,8},{10,11... | collective-permute-start | bytes 184328 | tf_op jit(solution)/shard_map/ppermute | solution.py:153
  50.1 1.5 %collective-permute-start.20 = (bf16[40,768]{1,0:T(8,128)(2,1)S(1)}, bf16[40,768]{1,0:T(8,128)(2,1)S(1)}, u32[]{:S(2)}, u32[]{:S(2)}) collective-permute-start(bf16[40,768]{1,0:T(8,128)(2,1)S(1)} %get-tuple-element.60), channel_id=1, source_target_pairs={{0,5},{1,4},{2,7},{3,6},{4,1},{5,0},{6,3},{7,2},{8,13},{9,12},{10,... | collective-permute-start | bytes 184328 | tf_op jit(solution)/shard_map/ppermute | solution.py:153
  51.6 0.5 collective-permute-start.18
  52.1 0.9 %collective-permute-done.19 = bf16[40,768]{1,0:T(8,128)(2,1)S(1)} collective-permute-done((bf16[40,768]{1,0:T(8,128)(2,1)S(1)}, bf16[40,768]{1,0:T(8,128)(2,1)S(1)}, u32[]{:S(2)}, u32[]{:S(2)}) %collective-permute-start.19) | collective-permute-done | bytes 61472 | tf_op jit(solution)/shard_map/ppermute | solution.py:153
  53.1 2.2 %collective-permute-done.20 = bf16[40,768]{1,0:T(8,128)(2,1)S(1)} collective-permute-done((bf16[40,768]{1,0:T(8,128)(2,1)S(1)}, bf16[40,768]{1,0:T(8,128)(2,1)S(1)}, u32[]{:S(2)}, u32[]{:S(2)}) %collective-permute-start.20) | collective-permute-done | bytes 61472 | tf_op jit(solution)/shard_map/ppermute | solution.py:153
  55.3 0.7 %collective-permute-done.18 = bf16[40,768]{1,0:T(8,128)(2,1)S(1)} collective-permute-done((bf16[40,768]{1,0:T(8,128)(2,1)S(1)}, bf16[40,768]{1,0:T(8,128)(2,1)S(1)}, u32[]{:S(2)}, u32[]{:S(2)}) %collective-permute-start.18) | collective-permute-done | bytes 61472 | tf_op jit(solution)/shard_map/ppermute | solution.py:153
  55.9 0.0 copy-done.2
  55.9 0.0 copy-done.3
  55.9 0.8 %multiply_subtract_fusion = (f32[40,768]{1,0:T(8,128)}, f32[40,768]{1,0:T(8,128)}) fusion(f32[40,768]{1,0:T(8,128)S(1)} %copy-done.2, bf16[40,768]{1,0:T(8,128)(2,1)S(1)} %collective-permute-done.20, bf16[40,768]{1,0:T(8,128)(2,1)S(1)} %collective-permute-done.19, bf16[40,768]{1,0:T(8,128)(2,1)S(1)} %collective-permute-done.18, ...), kind=kLoop, calls=%fused_computation.8 | loop fusion | flops 460800 | bytes 798720 | tf_op jit(solution)/shard_map/sub | solution.py:250
  (13 shorter events, 0.3 us)
Async XLA Ops:
  1.5 9.2 %collective-permute-start.3 = (bf16[40,768]{1,0:T(8,128)(2,1)S(1)}, bf16[40,768]{1,0:T(8,128)(2,1)S(1)}, u32[]{:S(2)}, u32[]{:S(2)}) collective-permute-start(bf16[40,768]{1,0:T(8,128)(2,1)S(1)} %convert_element_type.31.refs_0_), channel_id=1, source_target_pairs={{0,24},{1,25},{2,26},{3,27},{4,28},{5,29},{6,30},{7,31},{8,16},{9,... | collective-permute-start | bytes 184328 | tf_op jit(solution)/shard_map/ppermute | solution.py:153
  6.6 5.3 %collective-permute-start.2 = (bf16[40,768]{1,0:T(8,128)(2,1)S(1)}, bf16[40,768]{1,0:T(8,128)(2,1)S(1)}, u32[]{:S(2)}, u32[]{:S(2)}) collective-permute-start(bf16[40,768]{1,0:T(8,128)(2,1)S(1)} %convert_element_type.31.refs_0_), channel_id=1, source_target_pairs={{0,16},{1,17},{2,18},{3,19},{4,20},{5,21},{6,22},{7,23},{8,24},{9,... | collective-permute-start | bytes 184328 | tf_op jit(solution)/shard_map/ppermute | solution.py:153
  6.6 5.3 %collective-permute-start.1 = (bf16[40,768]{1,0:T(8,128)(2,1)S(1)}, bf16[40,768]{1,0:T(8,128)(2,1)S(1)}, u32[]{:S(2)}, u32[]{:S(2)}) collective-permute-start(bf16[40,768]{1,0:T(8,128)(2,1)S(1)} %convert_element_type.31.refs_0_), channel_id=1, source_target_pairs={{0,8},{1,9},{2,10},{3,11},{4,12},{5,13},{6,14},{7,15},{8,0},{9,1},... | collective-permute-start | bytes 184328 | tf_op jit(solution)/shard_map/ppermute | solution.py:153
  9.0 2.9 %copy-start.1 = (bf16[1,128,768]{2,1,0:T(8,128)(2,1)S(1)}, bf16[1,128,768]{2,1,0:T(8,128)(2,1)}, u32[]{:S(2)}) copy-start(bf16[1,128,768]{2,1,0:T(8,128)(2,1)} %param.6) | copy-start | bytes 589828
  9.0 7.9 %copy-start = (bf16[128,1536]{1,0:T(8,128)(2,1)S(1)}, bf16[128,1536]{1,0:T(8,128)(2,1)}, u32[]{:S(2)}) copy-start(bf16[128,1536]{1,0:T(8,128)(2,1)} %shard_map.77.own_ref) | copy-start | bytes 1179652
  9.0 12.3 %collective-permute-start = (bf16[128,1536]{1,0:T(8,128)(2,1)}, bf16[128,1536]{1,0:T(8,128)(2,1)S(1)}, u32[]{:S(2)}, u32[]{:S(2)}) collective-permute-start(bf16[128,1536]{1,0:T(8,128)(2,1)} %shard_map.77.own_ref), channel_id=1, source_target_pairs={{0,4},{1,5},{2,6},{3,7},{4,0},{5,1},{6,2},{7,3},{8,12},{9,13},{10,... | collective-permute-start | bytes 1179656 | tf_op jit(solution)/shard_map/ppermute | solution.py:153
  11.9 10.2 %collective-permute-start.12 = (bf16[128,768]{1,0:T(8,128)(2,1)S(1)}, bf16[128,768]{1,0:T(8,128)(2,1)S(1)}, u32[]{:S(2)}, u32[]{:S(2)}) collective-permute-start(bf16[128,768]{1,0:T(8,128)(2,1)S(1)} %bitcast.7), channel_id=1, source_target_pairs={{0,8},{1,9},{2,10},{3,11},{4,12},{5,13},{6,14},{7,15},{8,0},{9,1},... | collective-permute-start | bytes 589832 | tf_op jit(solution)/shard_map/ppermute | solution.py:153
  13.1 10.5 %collective-permute-start.11 = (bf16[128,768]{1,0:T(8,128)(2,1)S(1)}, bf16[128,768]{1,0:T(8,128)(2,1)S(1)}, u32[]{:S(2)}, u32[]{:S(2)}) collective-permute-start(bf16[128,768]{1,0:T(8,128)(2,1)S(1)} %bitcast.8), channel_id=1, source_target_pairs={{0,16},{1,17},{2,18},{3,19},{4,20},{5,21},{6,22},{7,23},{8,24},{9,... | collective-permute-start | bytes 589832 | tf_op jit(solution)/shard_map/ppermute | solution.py:153
  15.3 9.6 %collective-permute-start.6 = (bf16[4,40,768]{2,1,0:T(8,128)(2,1)S(1)}, bf16[4,40,768]{2,1,0:T(8,128)(2,1)S(1)}, u32[]{:S(2)}, u32[]{:S(2)}) collective-permute-start(bf16[4,40,768]{2,1,0:T(8,128)(2,1)S(1)} %shard_map.79), channel_id=1, source_target_pairs={{0,4},{1,5},{2,6},{3,7},{4,0},{5,1},{6,2},{7,3},{8,12},{9,13},{10,... | collective-permute-start | bytes 737288 | tf_op jit(solution)/shard_map/ppermute | solution.py:153
  16.9 8.1 %collective-permute-start.4 = (bf16[128,1536]{1,0:T(8,128)(2,1)S(1)}, bf16[128,1536]{1,0:T(8,128)(2,1)S(1)}, u32[]{:S(2)}, u32[]{:S(2)}) collective-permute-start(bf16[128,1536]{1,0:T(8,128)(2,1)S(1)} %copy-done), channel_id=1, source_target_pairs={{0,2},{1,3},{2,0},{3,1},{4,6},{5,7},{6,4},{7,5},{8,10},{9,11},{10,... | collective-permute-start | bytes 1179656 | tf_op jit(solution)/shard_map/ppermute | solution.py:153
  22.0 3.0 %collective-permute-start.5 = (bf16[128,1536]{1,0:T(8,128)(2,1)S(1)}, bf16[128,1536]{1,0:T(8,128)(2,1)S(1)}, u32[]{:S(2)}, u32[]{:S(2)}) collective-permute-start(bf16[128,1536]{1,0:T(8,128)(2,1)S(1)} %collective-permute-done.y_ref), channel_id=1, source_target_pairs={{0,2},{1,3},{2,0},{3,1},{4,6},{5,7},{6,4},{7,5},{8,10},{9,11},{10,... | collective-permute-start | bytes 1179656 | tf_op jit(solution)/shard_map/ppermute | solution.py:153
  23.8 7.1 %collective-permute-start.13 = (bf16[128,768]{1,0:T(8,128)(2,1)S(1)}, bf16[128,768]{1,0:T(8,128)(2,1)S(1)}, u32[]{:S(2)}, u32[]{:S(2)}) collective-permute-start(bf16[128,768]{1,0:T(8,128)(2,1)S(1)} %get-tuple-element.40.refs_1_), channel_id=1, source_target_pairs={{0,8},{1,9},{2,10},{3,11},{4,12},{5,13},{6,14},{7,15},{8,0},{9,1},... | collective-permute-start | bytes 589832 | tf_op jit(solution)/shard_map/ppermute | solution.py:153
  26.3 1.6 %collective-permute-start.8 = (bf16[80,768]{1,0:T(8,128)(2,1)S(1)}, bf16[80,768]{1,0:T(8,128)(2,1)S(1)}, u32[]{:S(2)}, u32[]{:S(2)}) collective-permute-start(bf16[80,768]{1,0:T(8,128)(2,1)S(1)} %get-tuple-element.57), channel_id=1, source_target_pairs={{0,2},{1,3},{2,0},{3,1},{4,6},{5,7},{6,4},{7,5},{8,10},{9,11},{10,... | collective-permute-start | bytes 368648 | tf_op jit(solution)/shard_map/ppermute | solution.py:153
  26.4 1.5 %collective-permute-start.7 = (bf16[80,768]{1,0:T(8,128)(2,1)S(1)}, bf16[80,768]{1,0:T(8,128)(2,1)S(1)}, u32[]{:S(2)}, u32[]{:S(2)}) collective-permute-start(bf16[80,768]{1,0:T(8,128)(2,1)S(1)} %get-tuple-element.58), channel_id=1, source_target_pairs={{0,2},{1,3},{2,0},{3,1},{4,6},{5,7},{6,4},{7,5},{8,10},{9,11},{10,... | collective-permute-start | bytes 368648 | tf_op jit(solution)/shard_map/ppermute | solution.py:153
  26.9 1.6 %collective-permute-start.10 = (bf16[80,768]{1,0:T(8,128)(2,1)S(1)}, bf16[80,768]{1,0:T(8,128)(2,1)S(1)}, u32[]{:S(2)}, u32[]{:S(2)}) collective-permute-start(bf16[80,768]{1,0:T(8,128)(2,1)S(1)} %get-tuple-element.55), channel_id=1, source_target_pairs={{0,2},{1,3},{2,0},{3,1},{4,6},{5,7},{6,4},{7,5},{8,10},{9,11},{10,... | collective-permute-start | bytes 368648 | tf_op jit(solution)/shard_map/ppermute | solution.py:153
  27.1 1.4 %collective-permute-start.9 = (bf16[80,768]{1,0:T(8,128)(2,1)S(1)}, bf16[80,768]{1,0:T(8,128)(2,1)S(1)}, u32[]{:S(2)}, u32[]{:S(2)}) collective-permute-start(bf16[80,768]{1,0:T(8,128)(2,1)S(1)} %get-tuple-element.56), channel_id=1, source_target_pairs={{0,2},{1,3},{2,0},{3,1},{4,6},{5,7},{6,4},{7,5},{8,10},{9,11},{10,... | collective-permute-start | bytes 368648 | tf_op jit(solution)/shard_map/ppermute | solution.py:153
  32.5 1.9 %collective-permute-start.14 = (bf16[320,768]{1,0:T(8,128)(2,1)S(1)}, bf16[320,768]{1,0:T(8,128)(2,1)S(1)}, u32[]{:S(2)}, u32[]{:S(2)}) collective-permute-start(bf16[320,768]{1,0:T(8,128)(2,1)S(1)} %get-tuple-element.45), channel_id=1, source_target_pairs={{0,2},{1,3},{2,0},{3,1},{4,6},{5,7},{6,4},{7,5},{8,10},{9,11},{10,... | collective-permute-start | bytes 1474568 | tf_op jit(solution)/shard_map/ppermute | solution.py:153
  34.6 21.3 %copy-start.2 = (f32[40,768]{1,0:T(8,128)S(1)}, f32[40,768]{1,0:T(8,128)}, u32[]{:S(2)}) copy-start(f32[40,768]{1,0:T(8,128)} %param.9) | copy-start | bytes 368644
  34.6 21.3 %copy-start.3 = (f32[40,768]{1,0:T(8,128)S(1)}, f32[40,768]{1,0:T(8,128)}, u32[]{:S(2)}) copy-start(f32[40,768]{1,0:T(8,128)} %param.10) | copy-start | bytes 368644
  34.6 7.5 %collective-permute-start.15 = (bf16[80,768]{1,0:T(8,128)(2,1)S(1)}, bf16[80,768]{1,0:T(8,128)(2,1)S(1)}, u32[]{:S(2)}, u32[]{:S(2)}) collective-permute-start(bf16[80,768]{1,0:T(8,128)(2,1)S(1)} %get-tuple-element.52), channel_id=1, source_target_pairs={{0,8},{1,9},{2,10},{3,11},{4,12},{5,13},{6,14},{7,15},{8,0},{9,1},... | collective-permute-start | bytes 368648 | tf_op jit(solution)/shard_map/ppermute | solution.py:153
  36.1 12.4 %collective-permute-start.17 = (bf16[80,768]{1,0:T(8,128)(2,1)S(1)}, bf16[80,768]{1,0:T(8,128)(2,1)S(1)}, u32[]{:S(2)}, u32[]{:S(2)}) collective-permute-start(bf16[80,768]{1,0:T(8,128)(2,1)S(1)} %get-tuple-element.53), channel_id=1, source_target_pairs={{0,16},{1,17},{2,18},{3,19},{4,20},{5,21},{6,22},{7,23},{8,24},{9,... | collective-permute-start | bytes 368648 | tf_op jit(solution)/shard_map/ppermute | solution.py:153
  38.7 9.8 %collective-permute-start.16 = (bf16[80,768]{1,0:T(8,128)(2,1)S(1)}, bf16[80,768]{1,0:T(8,128)(2,1)S(1)}, u32[]{:S(2)}, u32[]{:S(2)}) collective-permute-start(bf16[80,768]{1,0:T(8,128)(2,1)S(1)} %get-tuple-element.54), channel_id=1, source_target_pairs={{0,24},{1,25},{2,26},{3,27},{4,28},{5,29},{6,30},{7,31},{8,16},{9,... | collective-permute-start | bytes 368648 | tf_op jit(solution)/shard_map/ppermute | solution.py:153
  48.6 4.5 %collective-permute-start.19 = (bf16[40,768]{1,0:T(8,128)(2,1)S(1)}, bf16[40,768]{1,0:T(8,128)(2,1)S(1)}, u32[]{:S(2)}, u32[]{:S(2)}) collective-permute-start(bf16[40,768]{1,0:T(8,128)(2,1)S(1)} %get-tuple-element.59), channel_id=1, source_target_pairs={{0,1},{1,0},{2,3},{3,2},{4,5},{5,4},{6,7},{7,6},{8,9},{9,8},{10,11... | collective-permute-start | bytes 184328 | tf_op jit(solution)/shard_map/ppermute | solution.py:153
  50.1 5.1 %collective-permute-start.20 = (bf16[40,768]{1,0:T(8,128)(2,1)S(1)}, bf16[40,768]{1,0:T(8,128)(2,1)S(1)}, u32[]{:S(2)}, u32[]{:S(2)}) collective-permute-start(bf16[40,768]{1,0:T(8,128)(2,1)S(1)} %get-tuple-element.60), channel_id=1, source_target_pairs={{0,5},{1,4},{2,7},{3,6},{4,1},{5,0},{6,3},{7,2},{8,13},{9,12},{10,... | collective-permute-start | bytes 184328 | tf_op jit(solution)/shard_map/ppermute | solution.py:153
  51.6 4.3 %collective-permute-start.18 = (bf16[40,768]{1,0:T(8,128)(2,1)S(1)}, bf16[40,768]{1,0:T(8,128)(2,1)S(1)}, u32[]{:S(2)}, u32[]{:S(2)}) collective-permute-start(bf16[40,768]{1,0:T(8,128)(2,1)S(1)} %get-tuple-element.60), channel_id=1, source_target_pairs={{0,4},{1,5},{2,6},{3,7},{4,0},{5,1},{6,2},{7,3},{8,12},{9,13},{10,... | collective-permute-start | bytes 184328 | tf_op jit(solution)/shard_map/ppermute | solution.py:153
